TPU v7x, 32 devices: a whole 2x2x4 slice. The times are simulated.
32 devices in a mesh: ctx: 2 (over core), dp: 16 (over z, y, x).
Axes of the slice: x: 2, y: 2, z: 4, core: 2. Of those that a mesh axis runs over, the one named last changes fastest.
Arguments:
- inputs: bfloat16 [16, 256, 2048], P('dp', 'ctx'), may hold values from -8 to 8
- values: bfloat16 [16, 256, 2048], P('dp', 'ctx'), may hold values from -6 to 6
- gating: bfloat16 [16, 256, 2048], P('dp', 'ctx'), may hold values from -6 to 6
- out_grad: bfloat16 [16, 256, 2048], P('dp', 'ctx'), may hold values from -6 to 6
- weight: bfloat16 [2048, 2048], P('dp'), may hold values from -0.125 to 0.125
- decay_rate: float32 [16, 2048], replicated, may hold values from 0.001953125 to 0.08
- mode_gain: float32 [16, 2048], replicated, may hold values from -1.75 to 1.75
Outputs:
- in_grad: float32 [16, 256, 2048], P('dp', 'ctx')
- gate_grad: float32 [16, 256, 2048], P('dp', 'ctx')
- weight_grad: float32 [2048, 2048], P('dp')
All inputs are finite; a program needn't handle non-finite values.
Results may differ from a plain program's by a relative error of at most 0.003.
Values may be sent and summed in bfloat16 or wider, within the bound.
A program may use at most 128 MiB of HBM per device.

v0:
```python
import math

import jax
import jax.numpy as jnp
from jax import lax
from jax.sharding import PartitionSpec as P


def passed_along(block, axis, distance):
    devices = range(lax.axis_size(axis))
    route = [(i - distance, i) for i in devices if i - distance in devices]
    return lax.ppermute(block, axis, route)


def chain_combine(earlier, later):
    return (later[0] + later[1] * earlier[0], earlier[1] * later[1])


def power_rows(decay_rate, row_count, offset):
    steps = jnp.arange(row_count, dtype=jnp.float32) + offset
    return jnp.exp(-decay_rate[None, :, :] * steps[:, None, None])


def modal_tables(decay_rate, mode_gain, block_len):
    mode_coef = mode_gain * jnp.sqrt(-jnp.expm1(-2.0 * decay_rate))
    power_table = power_rows(decay_rate, block_len, 0.0)
    impulse = jnp.sum(mode_coef[None] * power_table, axis=1)
    sum_weights = power_table[::-1]
    inject_table = mode_coef[None] * power_rows(decay_rate, block_len, 1.0)
    step_decay = jnp.exp(-decay_rate * block_len)
    return (impulse, sum_weights, inject_table, step_decay)


def local_pass(series, tables):
    impulse, sum_weights, inject_table, step_decay = tables
    block_len = impulse.shape[0]
    mode_count = sum_weights.shape[1]
    blocked = series.reshape(-1, block_len, series.shape[-1])
    within_block = impulse[0][None, None, :] * blocked
    for lag_step in range(1, block_len):
        shifted = jnp.pad(blocked[:, : block_len - lag_step], ((0, 0), (lag_step, 0), (0, 0)))
        within_block = within_block + impulse[lag_step][None, None, :] * shifted
    block_sums = jnp.zeros((blocked.shape[0], mode_count, blocked.shape[2]), jnp.float32)
    for row_step in range(block_len):
        block_sums = block_sums + sum_weights[row_step][None] * blocked[:, row_step][:, None, :]
    block_decay = jnp.broadcast_to(step_decay, block_sums.shape)
    end_state, end_decay = lax.associative_scan(chain_combine, (block_sums, block_decay), axis=0)
    return (within_block, end_state, end_decay)


def finish_pass(within_block, end_state, end_decay, incoming, inject_table):
    total_state = end_state + end_decay * incoming[None]
    prior_state = jnp.concatenate([incoming[None], total_state[:-1]], axis=0)
    carried = within_block
    for mode_step in range(inject_table.shape[1]):
        carried = carried + inject_table[:, mode_step][None] * prior_state[:, mode_step][:, None, :]
    return carried.reshape(-1, within_block.shape[-1])


def entering(fwd_own, fwd_span, back_own, back_span):
    empty_state = jnp.zeros_like(fwd_own)
    n_ctx = lax.axis_size("ctx")

    def fwd_step(step_index, loop_state):
        received = passed_along(loop_state[1], "ctx", 1)
        return (received, fwd_own + fwd_span * received)

    def back_step(step_index, loop_state):
        received = passed_along(loop_state[1], "ctx", -1)
        return (received, back_own + back_span * received)

    fwd_in = lax.fori_loop(0, n_ctx - 1, fwd_step, (empty_state, fwd_own))[0]
    back_in = lax.fori_loop(0, n_ctx - 1, back_step, (empty_state, back_own))[0]
    return (fwd_in, back_in)


def on_device(inputs, values, gating, out_grad, weight, decay_rate, mode_gain):
    in_rows = inputs[0]
    tok_rows = in_rows.shape[0]
    n_ctx = lax.axis_size("ctx")
    n_dp = lax.axis_size("dp")
    tables = modal_tables(decay_rate, mode_gain, 16)
    fwd_within, fwd_end, fwd_decay = local_pass(values[0].astype(jnp.float32), tables)
    mix_grad = gating[0].astype(jnp.float32) * out_grad[0].astype(jnp.float32)
    back_within, back_end, back_decay = local_pass(jnp.flip(mix_grad, 0), tables)
    fwd_in, back_in = entering(fwd_end[-1], fwd_decay[-1], back_end[-1], back_decay[-1])
    val_grad = jnp.flip(
        finish_pass(back_within, back_end, back_decay, back_in, tables[2]), 0
    ).astype(jnp.bfloat16)
    mixed = finish_pass(fwd_within, fwd_end, fwd_decay, fwd_in, tables[2])
    gate_grad = out_grad[0].astype(jnp.float32) * mixed
    in_grad = lax.dot_general(
        val_grad,
        lax.all_gather(weight, "dp", axis=0, tiled=True),
        (((1,), (1,)), ((), ())),
        preferred_element_type=jnp.float32,
    )
    norm_factor = 1.0 / math.sqrt(tok_rows * n_ctx * n_dp)
    share = lax.psum_scatter(
        norm_factor
        * lax.dot_general(
            in_rows, val_grad, (((0,), (0,)), ((), ())), preferred_element_type=jnp.float32
        ),
        "dp",
        scatter_dimension=0,
        tiled=True,
    )
    weight_grad = lax.psum(share, "ctx")
    return (in_grad[None], gate_grad[None], weight_grad)


def solution(mesh):
    placed = (
        P("dp", "ctx", None),
        P("dp", "ctx", None),
        P("dp", "ctx", None),
        P("dp", "ctx", None),
        P("dp", None),
        P(),
        P(),
    )
    return jax.shard_map(
        on_device,
        mesh=mesh,
        in_specs=placed,
        out_specs=(P("dp", "ctx", None), P("dp", "ctx", None), P("dp", None)),
        check_vma=False,
    )
```

profile of v0, /device:TPU:1, one launch (start us, length us, event | category | flops | bytes accessed | tf_op | source)
XLA Modules:
  0.0 613.8 jit_solution(14980827042316583077)
XLA Ops:
  10.8 2.6 multiply_reduce_fusion
  22.1 2.4 pad.213
  24.6 2.5 pad.214
  27.0 2.4 pad.187
  29.4 1.7 pad_maximum_fusion.3
  31.1 2.4 pad.186
  35.2 2.4 pad.192
  39.1 2.0 add.493
  41.1 2.7 fusion.3
  44.7 4.1 pad.188
  48.8 4.1 pad.505
  54.6 2.6 collective-permute-start
  57.2 4.1 pad.235
  61.2 2.0 add.497
  68.8 1.9 fusion.48
  78.6 4.1 pad.194
  82.7 4.1 pad.195
  86.8 3.3 fusion.49
  94.6 5.0 multiply_add_fusion.2
  99.6 6.3 %rev.9 = bf16[128,2048]{1,0:T(8,128)(2,1)S(1)} reverse(bf16[128,2048]{1,0:T(8,128)(2,1)} %bitcast.320), dimensions={0} | reverse | bytes 1048576 | tf_op jit(solution)/shard_map/jit(_flip)/rev | solution.py:87
  105.9 8.2 %multiply_bitcast_fusion = f32[2048,2048]{0,1:T(8,128)} fusion(bf16[1,128,2048]{2,1,0:T(8,128)(2,1)S(1)} %copy-done, bf16[128,2048]{1,0:T(8,128)(2,1)S(1)} %rev.9), kind=kOutput, calls=%fused_computation | convolution fusion | flops 1077936128 | bytes 17825792 | tf_op jit(solution)/shard_map/dot_general | solution.py:101
  116.9 2.0 pad.506
  120.0 2.3 pad.215
  124.8 2.3 pad.241
  127.1 2.3 pad.239
  134.7 5.1 multiply_add_fusion
  139.8 323.1 %reduce-scatter.2.cloned.1.call-done = f32[128,2048]{0,1:T(8,128)} async-done(((f32[2048,2048]{0,1:T(8,128)}), f32[128,2048]{0,1:T(8,128)}) %reduce-scatter.2.cloned.1.call-update) | async-done | bytes 1048592 | tf_op jit(solution)/shard_map/reduce_scatter | solution.py:99
  463.0 2.3 convert_multiply_fusion
  465.3 118.1 %all-gather.2.cloned.1.call-done = bf16[2048,2048]{1,0:T(8,128)(2,1)} async-done(((bf16[128,2048]{1,0:T(8,128)(2,1)}), bf16[2048,2048]{1,0:T(8,128)(2,1)}) %all-gather.2.cloned.1.call-update) | async-done | bytes 8388624 | tf_op jit(solution)/shard_map/all_gather | solution.py:94
  583.4 7.3 %convolution_bitcast_fusion = f32[1,128,2048]{2,1,0:T(8,128)} fusion(bf16[2048,2048]{1,0:T(8,128)(2,1)} %all-gather.2.cloned.1.call-done, bf16[128,2048]{1,0:T(8,128)(2,1)S(1)} %copy-done.6), kind=kOutput, calls=%fused_computation.31 | convolution fusion | flops 1073741824 | bytes 9961472 | tf_op jit(solution)/shard_map/dot_general | solution.py:92
  590.7 14.0 %all-reduce.50.cloned.1.call-done = f32[128,2048]{0,1:T(8,128)} async-done(((f32[128,2048]{0,1:T(8,128)}), f32[128,2048]{0,1:T(8,128)}) %all-reduce.50.cloned.1.call-update) | async-done | bytes 1048592 | tf_op jit(solution)/shard_map/psum | solution.py:108
  604.7 2.5 copy.10
  (307 shorter events, 45.7 us)
Async XLA Ops:
  7.2 98.8 %copy-start = (bf16[1,128,2048]{2,1,0:T(8,128)(2,1)S(1)}, bf16[1,128,2048]{2,1,0:T(8,128)(2,1)}, u32[]{:S(2)}) copy-start(bf16[1,128,2048]{2,1,0:T(8,128)(2,1)} %param.7) | copy-start | bytes 1572868
  7.2 455.8 %reduce-scatter.2.cloned.1.call-start = ((), (), s32[]{:S(2)}) async-start(), calls=%async_computation.2 | async-start | bytes 17825792 | tf_op jit(solution)/shard_map/reduce_scatter | solution.py:99
  10.0 5.3 copy-start.59
  10.8 8.0 %copy-start.54 = (f32[16,2048]{1,0:T(8,128)}, f32[16,2048]{1,0:T(8,128)S(1)}, u32[]{:S(2)}) copy-start(f32[16,2048]{1,0:T(8,128)S(1)} %get-tuple-element.175) | copy-start | bytes 393220
  54.6 32.2 %collective-permute-start = (f32[16,2048]{1,0:T(8,128)}, f32[16,2048]{1,0:T(8,128)}, u32[]{:S(2)}, u32[]{:S(2)}) collective-permute-start(f32[16,2048]{1,0:T(8,128)} %add_bitcast_fusion.1), channel_id=1, source_target_pairs={{16,0},{17,1},{18,2},{19,3},{20,4},{21,5},{22,6},{23,7},{24,8},{25... | collective-permute-start | bytes 393224 | tf_op jit(solution)/shard_map/while/body/eval_jaxpr/ppermute | solution.py:12
  64.1 4.7 copy-start.3
  71.5 6.3 %copy-start.21 = (f32[3,16,2048]{2,1,0:T(8,128)S(1)}, f32[3,16,2048]{2,1,0:T(8,128)}, u32[]{:S(2)}) copy-start(f32[3,16,2048]{2,1,0:T(8,128)} %get-tuple-element.146) | copy-start | bytes 1179652
  71.5 6.3 %copy-start.63 = (f32[1,16,2048]{2,1,0:T(8,128)S(1)}, f32[1,16,2048]{2,1,0:T(8,128)}, u32[]{:S(2)}) copy-start(f32[1,16,2048]{2,1,0:T(8,128)} %get-tuple-element.174) | copy-start | bytes 393220
  90.1 4.1 copy-start.50
  90.1 4.1 copy-start.52
  90.1 4.1 copy-start.55
  90.1 4.1 copy-start.56
  90.2 4.1 copy-start.61
  90.2 4.1 copy-start.73
  90.2 4.1 copy-start.75
  90.2 4.1 copy-start.77
  90.2 4.1 copy-start.79
  90.2 4.1 copy-start.81
  90.2 4.1 copy-start.83
  90.2 4.1 copy-start.85
  90.2 4.1 copy-start.87
  90.2 4.1 copy-start.89
  90.3 4.1 copy-start.91
  105.9 8.2 %copy-start.5 = (bf16[128,2048]{1,0:T(8,128)(2,1)}, bf16[128,2048]{1,0:T(8,128)(2,1)S(1)}, u32[]{:S(2)}) copy-start(bf16[128,2048]{1,0:T(8,128)(2,1)S(1)} %rev.9) | copy-start | bytes 1572868
  114.2 469.2 %all-gather.2.cloned.1.call-start = ((), (), s32[]{:S(2)}) async-start(), calls=%async_computation.1 | async-start | bytes 8912896 | tf_op jit(solution)/shard_map/all_gather | solution.py:94
  114.9 489.8 %all-reduce.50.cloned.1.call-start = ((), (), s32[]{:S(2)}) async-start(), calls=%async_computation.3 | async-start | bytes 2097152 | tf_op jit(solution)/shard_map/psum | solution.py:108
  118.8 8.3 %copy-start.8 = (f32[8,16,2048]{2,1,0:T(8,128)}, f32[8,16,2048]{2,1,0:T(8,128)S(1)}, u32[]{:S(2)}) copy-start(f32[8,16,2048]{2,1,0:T(8,128)S(1)} %pad.506) | copy-start | bytes 3145732
  118.9 8.3 %copy-start.7 = (f32[4,16,2048]{2,1,0:T(8,128)S(1)}, f32[4,16,2048]{2,1,0:T(8,128)}, u32[]{:S(2)}) copy-start(f32[4,16,2048]{2,1,0:T(8,128)} %pad_maximum_fusion.1) | copy-start | bytes 1572868
  123.3 7.2 %collective-permute-start.1 = (f32[16,2048]{1,0:T(8,128)S(1)}, f32[16,2048]{1,0:T(8,128)S(1)}, u32[]{:S(2)}, u32[]{:S(2)}) collective-permute-start(f32[16,2048]{1,0:T(8,128)S(1)} %add_bitcast_fusion), channel_id=1, source_target_pairs={{0,16},{1,17},{2,18},{3,19},{4,20},{5,21},{6,22},{7,23},{8,24},{9,... | collective-permute-start | bytes 393224 | tf_op jit(solution)/shard_map/while/body/eval_jaxpr/ppermute | solution.py:12
  134.7 328.3 %copy-start.20 = (bf16[1,128,2048]{2,1,0:T(8,128)(2,1)S(1)}, bf16[1,128,2048]{2,1,0:T(8,128)(2,1)}, u32[]{:S(2)}) copy-start(bf16[1,128,2048]{2,1,0:T(8,128)(2,1)} %param.10) | copy-start | bytes 1572868
  139.8 443.6 %copy-start.6 = (bf16[128,2048]{1,0:T(8,128)(2,1)S(1)}, bf16[128,2048]{1,0:T(8,128)(2,1)}, u32[]{:S(2)}) copy-start(bf16[128,2048]{1,0:T(8,128)(2,1)} %copy-done.5) | copy-start | bytes 1572868
  583.4 23.9 %copy-start.1 = (bf16[1,128,2048]{2,1,0:T(8,128)(2,1)S(1)}, bf16[1,128,2048]{2,1,0:T(8,128)(2,1)}, u32[]{:S(2)}) copy-start(bf16[1,128,2048]{2,1,0:T(8,128)(2,1)} %param.7) | copy-start | bytes 1572868
  (67 other events, 122.9 us)
Sparse Core Ops, SparseCore 0:
  114.3 348.5 reduce-scatter.1
  465.7 117.6 all-gather.1
  585.8 18.9 all-reduce.49
where the time goes:
time: 616 us; the launch traced here: 614 us
  waiting for transfers between devices  456 us (74%)
  local copies, waits for them, and re-layouts  75.5 us (12%)
  other arithmetic  47 us (8%)
  matrix products  15.5 us (3%)
  between operations  15.5 us (3%)
    reduce_scatter x1, waiting for transfers between devices, on_device(): lax.psum_scatter(norm_factor * lax.dot_general(in_rows, val_grad, (((0,),...  323 us
    all_gather x1, waiting for transfers between devices, on_device(): lax.all_gather(weight, 'dp', axis=0, tiled=True)  118 us
    pad x10, local copies, waits for them, and re-layouts, local_pass(): lax.associative_scan(chain_combine, (block_sums, block_decay), axis=0)  28.3 us
    unnamed x245, local copies, waits for them, and re-layouts  20.1 us
    psum x1, waiting for transfers between devices, on_device(): weight_grad = lax.psum(share, 'ctx')  14 us
  transfers between devices with their start and end apart: 5, of which 3 were waited for; matrix products, arithmetic and copies ran while one was open for 10% of the time, Pallas kernels for 0%

commit v1 on v0

--- a/solution.py
+++ b/solution.py
@@ -1,9 +1,406 @@
+import functools
 import math
 
 import jax
 import jax.numpy as jnp
 from jax import lax
+from jax.experimental import pallas as pl
+from jax.experimental.pallas import tpu as pltpu
 from jax.sharding import PartitionSpec as P
+
+MESH = pl.DeviceIdType.MESH
+F32 = jnp.float32
+BF16 = jnp.bfloat16
+LANES = 128
+RUN = 16
+RUNS = 8
+ROWS = RUN * RUNS
+NZ = 4
+
+IN_COPY, BACK_COPY, FWD_COPY, VAL_COPY, IG_COPY, WG_COPY = range(6)
+AG_Z, AG_X, AG_Y, AG_A, AG_B, RS_A, RS_B, RS_X, RS_Y, RS_Z = range(6, 46, 4)
+COPIES = 46
+
+
+def dot(lhs, rhs, lhs_dim, rhs_dim):
+    return lax.dot_general(
+        lhs, rhs, (((lhs_dim,), (rhs_dim,)), ((), ())), preferred_element_type=F32
+    )
+
+
+def lanes_of(tile):
+    return pl.ds(pl.multiple_of(tile * LANES, LANES), LANES)
+
+
+def run_rows(step):
+    return pl.ds(step, RUNS, RUN)
+
+
+def row_index():
+    return lax.broadcasted_iota(jnp.int32, (RUNS, LANES), 0)
+
+
+def shifted_runs(state, by, reverse):
+    rows = row_index()
+    if reverse:
+        return jnp.where(rows < RUNS - by, pltpu.roll(state, RUNS - by, 0), 0.0)
+    return jnp.where(rows >= by, pltpu.roll(state, by, 0), 0.0)
+
+
+def spread(row):
+    return jnp.broadcast_to(row, (RUNS, LANES))
+
+
+def modes_of(decay_ref, coef_ref, tile):
+    decay = decay_ref[:, lanes_of(tile)]
+    lam = jnp.exp(-decay)
+    coef = coef_ref[:, lanes_of(tile)]
+    return decay, lam, coef
+
+
+def run_states(series, decay, lam, states, ends, tile, reverse):
+    order = range(RUN - 1, -1, -1) if reverse else range(RUN)
+    steps = [series[tile, run_rows(step), :] for step in order]
+    over_run = jnp.exp(-float(RUN) * decay)
+    for mode in range(decay.shape[0]):
+        rate = spread(lam[mode : mode + 1])
+        state = steps[0]
+        for column in steps[1:]:
+            state = rate * state + column
+        span = spread(over_run[mode : mode + 1])
+        for by in (1, 2, 4):
+            state = state + span * shifted_runs(state, by, reverse)
+            span = span * span
+        states[tile, mode] = state
+        last = 0 if reverse else RUNS - 1
+        ends[tile, mode : mode + 1, :] = state[last : last + 1]
+
+
+def run_outputs(series, impulse, decay, lam, coef, states, incoming, enters, result, tile, reverse):
+    order = list(range(RUN - 1, -1, -1) if reverse else range(RUN))
+    steps = [series[tile, run_rows(step), :] for step in order]
+    lags = [spread(impulse[tile, lag : lag + 1, :]) for lag in range(RUN)]
+    ahead = row_index()
+    ahead = (RUNS - 1 - ahead if reverse else ahead).astype(F32) * float(RUN)
+    rates, carried = [], []
+    for mode in range(decay.shape[0]):
+        rate = spread(lam[mode : mode + 1])
+        entry = jnp.where(enters, spread(incoming[tile, mode : mode + 1, :]), 0.0)
+        prior = shifted_runs(states[tile, mode], 1, reverse)
+        prior = prior + jnp.exp(-ahead * spread(decay[mode : mode + 1])) * entry
+        rates.append(rate)
+        carried.append(spread(coef[mode : mode + 1]) * rate * prior)
+    for at, step in enumerate(order):
+        terms = [lags[at - back] * steps[back] for back in range(at + 1)] + carried
+        while len(terms) > 1:
+            odd = terms[-1:] if len(terms) % 2 else []
+            terms = [a + b for a, b in zip(terms[::2], terms[1::2])] + odd
+        result[tile, run_rows(step), :] = terms[0]
+        carried = [rate * item for rate, item in zip(rates, carried)]
+
+
+def chip_kernel(
+    scale,
+    in_ref, values_ref, gating_ref, grad_ref, weight_ref, decay_ref, coef_ref,
+    ig_ref, gate_ref, wg_ref,
+    series_f, series_b, result, impulse, states_f, states_b,
+    ends_f, ends_b, enter_f, enter_b,
+    in_full, val_full, val_send, wfull,
+    s1, r1a, r1b, s2x, s2y, r2x, r2y, s3, r3,
+    ig_send, ig_recv, wg_send, wg_recv,
+    send_sem, recv_sem,
+):
+    core = lax.axis_index("ctx")
+    dp = lax.axis_index("dp")
+    z, y, x = dp // 4, (dp // 2) % 2, dp % 2
+    tiles = series_f.shape[0]
+    half_tiles = tiles // 2
+    half = half_tiles * LANES
+    block = weight_ref.shape[0]
+    mid = block // 2
+
+    def chip(cz, cy, cx):
+        return cz * 4 + cy * 2 + cx
+
+    sibling = (1 - core, dp)
+    x_dev = (core, chip(z, y, 1 - x))
+    y_dev = (core, chip(z, 1 - y, x))
+
+    def z_dev(hop):
+        return (core, chip((z + hop) % NZ, y, x))
+
+    def copy(src, dst, which, device):
+        return pltpu.make_async_remote_copy(
+            src_ref=src, dst_ref=dst, send_sem=send_sem.at[which], recv_sem=recv_sem.at[which],
+            device_id=device, device_id_type=MESH,
+        )
+
+    barrier = pltpu.get_barrier_semaphore()
+    partners = [sibling, x_dev, y_dev] + [z_dev(hop) for hop in range(1, NZ)]
+    for device in partners:
+        pl.semaphore_signal(barrier, inc=1, device_id=device, device_id_type=MESH)
+    pl.semaphore_wait(barrier, len(partners))
+
+    def wrows(index, start=0, size=block):
+        return wfull.at[pl.ds(pl.multiple_of(index * block + start, mid), size), :]
+
+    own_half = pl.ds(pl.multiple_of(core * half, half), half)
+    other_half = pl.ds(pl.multiple_of((1 - core) * half, half), half)
+    own_rows = pl.ds(pl.multiple_of(core * ROWS, ROWS), ROWS)
+
+    wrows(dp)[...] = weight_ref[:, own_half]
+
+    def ag_z(hop):
+        return copy(wrows(dp), wrows(dp), AG_Z + hop, z_dev(hop))
+
+    def ag_x(hop):
+        rows = wrows(chip((z - hop + NZ) % NZ, y, x))
+        return copy(rows, rows, AG_X + hop, x_dev)
+
+    def ag_y(hop):
+        rows = wrows(chip((z - hop + NZ) % NZ, y, x))
+        return copy(rows, rows, AG_Y + hop, y_dev)
+
+    def ag_a(hop):
+        rows = wrows(chip((z - hop + NZ) % NZ, y, 1 - x), 0, mid)
+        return copy(rows, rows, AG_A + hop, y_dev)
+
+    def ag_b(hop):
+        rows = wrows(chip((z - hop + NZ) % NZ, 1 - y, x), mid, mid)
+        return copy(rows, rows, AG_B + hop, x_dev)
+
+    for hop in (1, 3, 2):
+        ag_z(hop).start()
+    ag_x(0).start()
+    ag_y(0).start()
+    in_copy = copy(in_ref, in_full.at[own_rows, :], IN_COPY, sibling)
+    in_copy.start()
+    in_full[own_rows, :] = in_ref[...]
+
+    def back_states(tile, carry):
+        lanes = lanes_of(tile)
+        series_b[tile] = gating_ref[:, lanes].astype(F32) * grad_ref[:, lanes].astype(F32)
+        decay, lam, coef = modes_of(decay_ref, coef_ref, tile)
+        power = coef
+        for lag in range(RUN):
+            impulse[tile, lag : lag + 1, :] = jnp.sum(power, axis=0, keepdims=True)
+            power = power * lam
+        run_states(series_b, decay, lam, states_b, ends_b, tile, True)
+        return carry
+
+    def fwd_states(tile, carry):
+        series_f[tile] = values_ref[:, lanes_of(tile)].astype(F32)
+        decay, lam, coef = modes_of(decay_ref, coef_ref, tile)
+        run_states(series_f, decay, lam, states_f, ends_f, tile, False)
+        return carry
+
+    lax.fori_loop(0, tiles, back_states, 0)
+    back_copy = copy(ends_b, enter_b, BACK_COPY, sibling)
+    back_copy.start()
+    lax.fori_loop(0, tiles, fwd_states, 0)
+    fwd_copy = copy(ends_f, enter_f, FWD_COPY, sibling)
+    fwd_copy.start()
+    back_copy.wait_recv()
+
+    def val_tile(tile):
+        decay, lam, coef = modes_of(decay_ref, coef_ref, tile)
+        run_outputs(
+            series_b, impulse, decay, lam, coef, states_b, enter_b, core == 0, result, tile, True
+        )
+        return result[tile].astype(BF16)
+
+    def val_other(tile, carry):
+        val_send[:, lanes_of(tile)] = val_tile((1 - core) * half_tiles + tile)
+        return carry
+
+    def val_own(tile, carry):
+        val_full[own_rows, lanes_of(tile)] = val_tile(core * half_tiles + tile)
+        return carry
+
+    lax.fori_loop(0, half_tiles, val_other, 0)
+    val_copy = copy(val_send, val_full.at[own_rows, :], VAL_COPY, sibling)
+    val_copy.start()
+    lax.fori_loop(0, half_tiles, val_own, 0)
+    in_copy.wait_recv()
+    val_copy.wait_recv()
+
+    def term(index):
+        columns = pl.ds(pl.multiple_of(index * block, block), block)
+        return dot(in_full[:, columns], val_full[...], 0, 0)
+
+    def rs_a(hop):
+        return copy(s1.at[hop, pl.ds(0, mid), :], r1a.at[hop], RS_A + hop, y_dev)
+
+    def rs_b(hop):
+        return copy(s1.at[hop, pl.ds(mid, mid), :], r1b.at[hop], RS_B + hop, x_dev)
+
+    def rs_x(hop):
+        return copy(s2x.at[hop], r2x.at[hop], RS_X + hop, x_dev)
+
+    def rs_y(hop):
+        return copy(s2y.at[hop], r2y.at[hop], RS_Y + hop, y_dev)
+
+    def rs_z(hop):
+        return copy(s3.at[hop], r3.at[hop], RS_Z + hop, z_dev(hop))
+
+    def rs_first(hop, carry):
+        s1[hop] = term(chip((z + hop) % NZ, 1 - y, 1 - x)).astype(BF16)
+        rs_a(hop).start()
+        rs_b(hop).start()
+        return carry
+
+    lax.fori_loop(0, NZ, rs_first, 0)
+
+    def ag_second(hop, carry):
+        ag_z(hop).wait_recv()
+        ag_x(hop).start()
+        ag_y(hop).start()
+        return carry
+
+    def rs_second(hop, carry):
+        to_x = term(chip((z + hop) % NZ, y, 1 - x))
+        rs_a(hop).wait_recv()
+        s2x[hop, pl.ds(0, mid), :] = (to_x[:mid] + r1a[hop].astype(F32)).astype(BF16)
+        s2x[hop, pl.ds(mid, mid), :] = to_x[mid:].astype(BF16)
+        rs_x(hop).start()
+        to_y = term(chip((z + hop) % NZ, 1 - y, x))
+        rs_b(hop).wait_recv()
+        s2y[hop, pl.ds(0, mid), :] = to_y[:mid].astype(BF16)
+        s2y[hop, pl.ds(mid, mid), :] = (to_y[mid:] + r1b[hop].astype(F32)).astype(BF16)
+        rs_y(hop).start()
+        return carry
+
+    lax.fori_loop(0, NZ, rs_second, 0)
+    lax.fori_loop(1, NZ, ag_second, 0)
+
+    fwd_copy.wait_recv()
+
+    def gate_tile(tile, carry):
+        decay, lam, coef = modes_of(decay_ref, coef_ref, tile)
+        run_outputs(
+            series_f, impulse, decay, lam, coef, states_f, enter_f, core == 1, result, tile, False
+        )
+        lanes = lanes_of(tile)
+        gate_ref[:, lanes] = grad_ref[:, lanes].astype(F32) * result[tile]
+        return carry
+
+    lax.fori_loop(0, tiles, gate_tile, 0)
+
+    def ag_third(hop, carry):
+        ag_x(hop).wait_recv()
+        ag_a(hop).start()
+        ag_y(hop).wait_recv()
+        ag_b(hop).start()
+        return carry
+
+    def own_sum(hop):
+        total = term(chip((z + hop) % NZ, y, x))
+        rs_x(hop).wait_recv()
+        rs_y(hop).wait_recv()
+        return total + r2x[hop].astype(F32) + r2y[hop].astype(F32)
+
+    def rs_third(hop, carry):
+        s3[hop] = own_sum(hop).astype(BF16)
+        rs_z(hop).start()
+        return carry
+
+    wg_send[...] = own_sum(0)
+    lax.fori_loop(1, NZ, rs_third, 0)
+    lax.fori_loop(0, NZ, ag_third, 0)
+
+    for hop in range(1, NZ):
+        rs_z(hop).wait_recv()
+        wg_send[...] += r3[hop].astype(F32)
+    wg_send[...] = scale * wg_send[...]
+    wg_copy = copy(wg_send, wg_recv, WG_COPY, sibling)
+    wg_copy.start()
+    wg_ref[:, own_half] = wg_send[...]
+
+    def ig_part(hop, carry):
+        cz = (z - hop + NZ) % NZ
+        ag_a(hop).wait_recv()
+        ag_b(hop).wait_recv()
+        for cy in range(2):
+            first = pl.multiple_of(chip(cz, cy, 0) * block, 2 * block)
+            part = dot(val_full[...], wfull[pl.ds(first, 2 * block), :], 1, 1)
+            columns = pl.ds(first, 2 * block)
+            top, bottom = part[:ROWS], part[ROWS:]
+            ig_ref[:, columns] = jnp.where(core == 0, top, bottom)
+            ig_send[:, columns] = jnp.where(core == 0, bottom, top)
+        return carry
+
+    lax.fori_loop(0, NZ, ig_part, 0)
+    ig_copy = copy(ig_send, ig_recv, IG_COPY, sibling)
+    ig_copy.start()
+    wg_copy.wait_recv()
+    wg_ref[:, other_half] = wg_recv[...]
+    ig_copy.wait_recv()
+    ig_ref[...] += ig_recv[...]
+
+    for single in (in_copy, back_copy, fwd_copy, val_copy, wg_copy, ig_copy):
+        single.wait_send()
+
+    def drain(hop, carry):
+        for each in (ag_x, ag_y, ag_a, ag_b, rs_a, rs_b, rs_x, rs_y):
+            each(hop).wait_send()
+        return carry
+
+    def drain_z(hop, carry):
+        ag_z(hop).wait_send()
+        rs_z(hop).wait_send()
+        return carry
+
+    lax.fori_loop(0, NZ, drain, 0)
+    lax.fori_loop(1, NZ, drain_z, 0)
+
+
+def on_chip_grid(inputs, values, gating, out_grad, weight, decay_rate, mode_gain):
+    rows, width = inputs.shape[1:]
+    channels = values.shape[2]
+    modes = decay_rate.shape[0]
+    block = weight.shape[0]
+    tiles, half, mid = channels // LANES, channels // 2, block // 2
+    scale = 1.0 / math.sqrt(rows * lax.axis_size("ctx") * lax.axis_size("dp"))
+    vmem = pl.BlockSpec(memory_space=pltpu.VMEM)
+    series = pltpu.VMEM((tiles, rows, LANES), F32)
+    states = pltpu.VMEM((tiles, modes, RUNS, LANES), F32)
+    ends = pltpu.VMEM((tiles, modes, LANES), F32)
+    blocks = pltpu.VMEM((NZ, block, half), BF16)
+    halves = pltpu.VMEM((NZ, mid, half), BF16)
+    mode_coef = mode_gain * jnp.sqrt(-jnp.expm1(-2.0 * decay_rate))
+    in_grad, gate_grad, weight_grad = pl.pallas_call(
+        functools.partial(chip_kernel, scale),
+        out_shape=(
+            jax.ShapeDtypeStruct((rows, width), F32),
+            jax.ShapeDtypeStruct((rows, channels), F32),
+            jax.ShapeDtypeStruct((block, channels), F32),
+        ),
+        in_specs=[vmem] * 7,
+        out_specs=(vmem,) * 3,
+        scratch_shapes=[
+            series, series, series, pltpu.VMEM((tiles, RUN, LANES), F32), states, states,
+            ends, ends, ends, ends,
+            pltpu.VMEM((2 * rows, width), BF16),
+            pltpu.VMEM((2 * rows, half), BF16),
+            pltpu.VMEM((rows, half), BF16),
+            pltpu.VMEM((width, half), BF16),
+            blocks, halves, halves, blocks, blocks, blocks, blocks, blocks, blocks,
+            pltpu.VMEM((rows, width), F32),
+            pltpu.VMEM((rows, width), F32),
+            pltpu.VMEM((block, half), F32),
+            pltpu.VMEM((block, half), F32),
+            pltpu.SemaphoreType.DMA((COPIES,)),
+            pltpu.SemaphoreType.DMA((COPIES,)),
+        ],
+        compiler_params=pltpu.CompilerParams(
+            collective_id=0, has_side_effects=True, vmem_limit_bytes=56 * 1024 * 1024
+        ),
+    )(inputs[0], values[0], gating[0], out_grad[0], weight, decay_rate, mode_coef)
+    return (in_grad[None], gate_grad[None], weight_grad)
+
+
+def fits_chip_grid(mesh):
+    return mesh.shape["ctx"] == 2 and mesh.shape["dp"] == 4 * NZ
 
 
 def passed_along(block, axis, distance):
@@ -119,8 +516,9 @@
         P(),
         P(),
     )
+    step = on_chip_grid if fits_chip_grid(mesh) else on_device
     return jax.shard_map(
-        on_device,
+        step,
         mesh=mesh,
         in_specs=placed,
         out_specs=(P("dp", "ctx", None), P("dp", "ctx", None), P("dp", None)),

time: 616 us -> 92.1 us (0.15)
  waiting for transfers between devices: 456 us -> 0 us
  Pallas kernels: 0 us -> 84.5 us
  local copies, waits for them, and re-layouts: 75.5 us -> 4.96 us
  other arithmetic: 47 us -> 1.71 us
  matrix products: 15.5 us -> 0 us
  between operations: 15.5 us -> 0.65 us
    reduce_scatter x1 -> x0, waiting for transfers between devices: 323 us -> none  [on_device(): lax.psum_scatter(norm_factor * lax.dot_general(in_rows, val_grad, (((0,),...]
    all_gather x1 -> x0, waiting for transfers between devices: 118 us -> none  [on_device(): lax.all_gather(weight, 'dp', axis=0, tiled=True)]
    pallas_call x0 -> x1, Pallas kernels: none -> 84.5 us  [on_chip_grid(): pl.pallas_call(functools.partial(chip_kernel, scale), out_shape=(jax.Shap...]
    pad x10 -> x0, local copies, waits for them, and re-layouts: 28.3 us -> none  [local_pass(): lax.associative_scan(chain_combine, (block_sums, block_decay), axis=0)]
    add x16 -> x0, other arithmetic: 22.4 us -> none  [the longest x2 10.2 us: finish_pass(): carried + inject_table[:, mode_step][None] * prior_state[:, mode_step][:,...]
    slice x31 -> x0, local copies, waits for them, and re-layouts: 20.1 us -> none  [the longest x3 8.65 us: finish_pass(): prior_state = jnp.concatenate([incoming[None], total_state[:-1]], axis=0)]
    dot_general x2 -> x0, matrix products: 15.5 us -> none  [the longest x1 8.22 us: on_device(): lax.dot_general(in_rows, val_grad, (((0,), (0,)), ((), ())), preferred_el...]
    unnamed x245 -> x7, local copies, waits for them, and re-layouts: 20.1 us -> 4.96 us
  transfers between devices with their start and end apart: 5 -> 0, of which waited for: 3 -> 0; matrix products, arithmetic and copies ran while one was open for 10% -> 0% of each run, Pallas kernels for 0% -> 0%
where the time goes in v1:
time: 92.1 us; the launch traced here: 91.8 us
  Pallas kernels  84.5 us (92%)
  local copies, waits for them, and re-layouts  4.96 us (5%)
  other arithmetic  1.71 us (2%)
    pallas_call x1, Pallas kernels, on_chip_grid(): pl.pallas_call(functools.partial(chip_kernel, scale), out_shape=(jax.Shap...  84.5 us
    unnamed x7, local copies, waits for them, and re-layouts  4.96 us

profile of v1, /device:TPU:1, one launch (start us, length us, event | category | flops | bytes accessed | tf_op | source)
XLA Modules:
  0.0 91.8 jit_solution(13268971646759422079)
XLA Ops:
  0.6 1.7 %sqrt_multiply_fusion.coef_ref = f32[16,2048]{1,0:T(8,128)} fusion(f32[16,2048]{1,0:T(8,128)} %param.13, f32[16,2048]{1,0:T(8,128)} %decay_ref.1), kind=kLoop, calls=%fused_computation | loop fusion | flops 98304 | bytes 393216 | tf_op jit(solution)/shard_map/mul | solution.py:370
  2.3 84.5 %shard_map.94 = (f32[128,2048]{1,0:T(8,128)}, f32[128,2048]{1,0:T(8,128)}, f32[128,2048]{1,0:T(8,128)}) custom-call(bf16[128,2048]{1,0:T(8,128)(2,1)} %bitcast.8, bf16[128,2048]{1,0:T(8,128)(2,1)} %bitcast.9, bf16[128,2048]{1,0:T(8,128)(2,1)} %bitcast.10, bf16[128,2048]{1,0:T(8,128)(2,1)} %bitcast.11, bf16[128,2048]{1,0:T(8,128)(2,1)} %weight_ref.1, ...), custom_call_target="tpu_custom_call" | custom-call | tf_op jit(solution)/shard_map/pallas_call | solution.py:371
  86.8 0.0 copy-start.1
  86.9 2.4 %copy.13 = f32[1,128,2048]{2,1,0:T(8,128)} copy(f32[1,128,2048]{2,1,0:T(8,128)} %bitcast.7) | data formatting | bytes 2097152
  89.2 0.0 copy-done.1
  89.2 0.0 copy-start
  89.2 1.0 %copy.14 = f32[1,128,2048]{2,1,0:T(8,128)} copy(f32[1,128,2048]{2,1,0:T(8,128)S(1)} %bitcast.6) | data formatting | bytes 2097152
  90.2 0.6 copy-done
  90.8 1.0 %copy.15 = f32[128,2048]{1,0:T(8,128)} copy(f32[128,2048]{1,0:T(8,128)S(1)} %copy-done) | data formatting | bytes 2097152
Async XLA Ops:
  86.8 2.4 %copy-start.1 = (f32[128,2048]{1,0:T(8,128)S(1)}, f32[128,2048]{1,0:T(8,128)}, u32[]{:S(2)}) copy-start(f32[128,2048]{1,0:T(8,128)} %get-tuple-element.7) | copy-start | bytes 3145732
  89.2 1.6 %copy-start = (f32[128,2048]{1,0:T(8,128)S(1)}, f32[128,2048]{1,0:T(8,128)}, u32[]{:S(2)}) copy-start(f32[128,2048]{1,0:T(8,128)} %get-tuple-element.14) | copy-start | bytes 3145732

commit v2 on v1

--- a/solution.py
+++ b/solution.py
@@ -17,9 +17,9 @@
 ROWS = RUN * RUNS
 NZ = 4
 
-IN_COPY, BACK_COPY, FWD_COPY, VAL_COPY, IG_COPY, WG_COPY = range(6)
-AG_Z, AG_X, AG_Y, AG_A, AG_B, RS_A, RS_B, RS_X, RS_Y, RS_Z = range(6, 46, 4)
-COPIES = 46
+IN_COPY, BACK_COPY, FWD_COPY, VAL_COPY, WG_COPY = range(5)
+AG_Z, AG_X, AG_Y, AG_A, AG_B, RS_A, RS_B, RS_X, RS_Y, RS_Z, IG_COPY = range(5, 49, 4)
+COPIES = 49
 
 
 def dot(lhs, rhs, lhs_dim, rhs_dim):
@@ -51,10 +51,17 @@
     return jnp.broadcast_to(row, (RUNS, LANES))
 
 
-def modes_of(decay_ref, coef_ref, tile):
+def one_less_exp(u):
+    series = 1.0
+    for order in range(8, 1, -1):
+        series = 1.0 - u * (1.0 / order) * series
+    return jnp.where(u > 0.25, 1.0 - jnp.exp(-u), u * series)
+
+
+def modes_of(decay_ref, gain_ref, tile):
     decay = decay_ref[:, lanes_of(tile)]
     lam = jnp.exp(-decay)
-    coef = coef_ref[:, lanes_of(tile)]
+    coef = gain_ref[:, lanes_of(tile)] * jnp.sqrt(one_less_exp(2.0 * decay))
     return decay, lam, coef
 
 
@@ -101,7 +108,7 @@
 
 def chip_kernel(
     scale,
-    in_ref, values_ref, gating_ref, grad_ref, weight_ref, decay_ref, coef_ref,
+    in_ref, values_ref, gating_ref, grad_ref, weight_ref, decay_ref, gain_ref,
     ig_ref, gate_ref, wg_ref,
     series_f, series_b, result, impulse, states_f, states_b,
     ends_f, ends_b, enter_f, enter_b,
@@ -169,8 +176,18 @@
         rows = wrows(chip((z - hop + NZ) % NZ, 1 - y, x), mid, mid)
         return copy(rows, rows, AG_B + hop, x_dev)
 
-    for hop in (1, 3, 2):
-        ag_z(hop).start()
+    def ag_second(hop):
+        ag_z(hop).wait_recv()
+        ag_x(hop).start()
+        ag_y(hop).start()
+
+    def ag_third(hop):
+        ag_x(hop).wait_recv()
+        ag_a(hop).start()
+        ag_y(hop).wait_recv()
+        ag_b(hop).start()
+
+    ag_z(1).start()
     ag_x(0).start()
     ag_y(0).start()
     in_copy = copy(in_ref, in_full.at[own_rows, :], IN_COPY, sibling)
@@ -180,7 +197,7 @@
     def back_states(tile, carry):
         lanes = lanes_of(tile)
         series_b[tile] = gating_ref[:, lanes].astype(F32) * grad_ref[:, lanes].astype(F32)
-        decay, lam, coef = modes_of(decay_ref, coef_ref, tile)
+        decay, lam, coef = modes_of(decay_ref, gain_ref, tile)
         power = coef
         for lag in range(RUN):
             impulse[tile, lag : lag + 1, :] = jnp.sum(power, axis=0, keepdims=True)
@@ -190,20 +207,23 @@
 
     def fwd_states(tile, carry):
         series_f[tile] = values_ref[:, lanes_of(tile)].astype(F32)
-        decay, lam, coef = modes_of(decay_ref, coef_ref, tile)
+        decay, lam, coef = modes_of(decay_ref, gain_ref, tile)
         run_states(series_f, decay, lam, states_f, ends_f, tile, False)
         return carry
 
     lax.fori_loop(0, tiles, back_states, 0)
     back_copy = copy(ends_b, enter_b, BACK_COPY, sibling)
     back_copy.start()
+    ag_z(3).start()
     lax.fori_loop(0, tiles, fwd_states, 0)
     fwd_copy = copy(ends_f, enter_f, FWD_COPY, sibling)
     fwd_copy.start()
+    ag_second(1)
+    ag_third(0)
     back_copy.wait_recv()
 
     def val_tile(tile):
-        decay, lam, coef = modes_of(decay_ref, coef_ref, tile)
+        decay, lam, coef = modes_of(decay_ref, gain_ref, tile)
         run_outputs(
             series_b, impulse, decay, lam, coef, states_b, enter_b, core == 0, result, tile, True
         )
@@ -221,6 +241,7 @@
     val_copy = copy(val_send, val_full.at[own_rows, :], VAL_COPY, sibling)
     val_copy.start()
     lax.fori_loop(0, half_tiles, val_own, 0)
+    ag_z(2).start()
     in_copy.wait_recv()
     val_copy.wait_recv()
 
@@ -243,21 +264,12 @@
     def rs_z(hop):
         return copy(s3.at[hop], r3.at[hop], RS_Z + hop, z_dev(hop))
 
-    def rs_first(hop, carry):
+    def rs_first(hop):
         s1[hop] = term(chip((z + hop) % NZ, 1 - y, 1 - x)).astype(BF16)
         rs_a(hop).start()
         rs_b(hop).start()
-        return carry
-
-    lax.fori_loop(0, NZ, rs_first, 0)
-
-    def ag_second(hop, carry):
-        ag_z(hop).wait_recv()
-        ag_x(hop).start()
-        ag_y(hop).start()
-        return carry
-
-    def rs_second(hop, carry):
+
+    def rs_second(hop):
         to_x = term(chip((z + hop) % NZ, y, 1 - x))
         rs_a(hop).wait_recv()
         s2x[hop, pl.ds(0, mid), :] = (to_x[:mid] + r1a[hop].astype(F32)).astype(BF16)
@@ -268,15 +280,15 @@
         s2y[hop, pl.ds(0, mid), :] = to_y[:mid].astype(BF16)
         s2y[hop, pl.ds(mid, mid), :] = (to_y[mid:] + r1b[hop].astype(F32)).astype(BF16)
         rs_y(hop).start()
-        return carry
-
-    lax.fori_loop(0, NZ, rs_second, 0)
-    lax.fori_loop(1, NZ, ag_second, 0)
+
+    for hop in (1, 2, 3, 0):
+        rs_first(hop)
+    ag_second(3)
 
     fwd_copy.wait_recv()
 
     def gate_tile(tile, carry):
-        decay, lam, coef = modes_of(decay_ref, coef_ref, tile)
+        decay, lam, coef = modes_of(decay_ref, gain_ref, tile)
         run_outputs(
             series_f, impulse, decay, lam, coef, states_f, enter_f, core == 1, result, tile, False
         )
@@ -286,12 +298,9 @@
 
     lax.fori_loop(0, tiles, gate_tile, 0)
 
-    def ag_third(hop, carry):
-        ag_x(hop).wait_recv()
-        ag_a(hop).start()
-        ag_y(hop).wait_recv()
-        ag_b(hop).start()
-        return carry
+    for hop in (1, 2, 3, 0):
+        rs_second(hop)
+    ag_second(2)
 
     def own_sum(hop):
         total = term(chip((z + hop) % NZ, y, x))
@@ -299,24 +308,27 @@
         rs_y(hop).wait_recv()
         return total + r2x[hop].astype(F32) + r2y[hop].astype(F32)
 
-    def rs_third(hop, carry):
+    def rs_third(hop):
         s3[hop] = own_sum(hop).astype(BF16)
         rs_z(hop).start()
-        return carry
-
+
+    rs_third(1)
+    ag_third(1)
+    rs_third(2)
+    ag_third(3)
+    rs_third(3)
     wg_send[...] = own_sum(0)
-    lax.fori_loop(1, NZ, rs_third, 0)
-    lax.fori_loop(0, NZ, ag_third, 0)
-
-    for hop in range(1, NZ):
-        rs_z(hop).wait_recv()
-        wg_send[...] += r3[hop].astype(F32)
-    wg_send[...] = scale * wg_send[...]
-    wg_copy = copy(wg_send, wg_recv, WG_COPY, sibling)
-    wg_copy.start()
-    wg_ref[:, own_half] = wg_send[...]
-
-    def ig_part(hop, carry):
+    ag_third(2)
+
+    def ig_columns(hop):
+        first = ((z - hop + NZ) % NZ) * 4 * block
+        return pl.ds(pl.multiple_of(first, 4 * block), 4 * block)
+
+    def ig_copy(hop):
+        columns = ig_columns(hop)
+        return copy(ig_send.at[:, columns], ig_recv.at[:, columns], IG_COPY + hop, sibling)
+
+    def ig_part(hop):
         cz = (z - hop + NZ) % NZ
         ag_a(hop).wait_recv()
         ag_b(hop).wait_recv()
@@ -327,21 +339,36 @@
             top, bottom = part[:ROWS], part[ROWS:]
             ig_ref[:, columns] = jnp.where(core == 0, top, bottom)
             ig_send[:, columns] = jnp.where(core == 0, bottom, top)
-        return carry
-
-    lax.fori_loop(0, NZ, ig_part, 0)
-    ig_copy = copy(ig_send, ig_recv, IG_COPY, sibling)
-    ig_copy.start()
+        ig_copy(hop).start()
+
+    def ig_finish(hop):
+        columns = ig_columns(hop)
+        ig_copy(hop).wait_recv()
+        ig_ref[:, columns] += ig_recv[:, columns]
+
+    ig_part(0)
+    ig_part(1)
+    ig_part(3)
+
+    for hop in range(1, NZ):
+        rs_z(hop).wait_recv()
+        wg_send[...] += r3[hop].astype(F32)
+    wg_send[...] = scale * wg_send[...]
+    wg_copy = copy(wg_send, wg_recv, WG_COPY, sibling)
+    wg_copy.start()
+    wg_ref[:, own_half] = wg_send[...]
+
+    ig_part(2)
     wg_copy.wait_recv()
     wg_ref[:, other_half] = wg_recv[...]
-    ig_copy.wait_recv()
-    ig_ref[...] += ig_recv[...]
-
-    for single in (in_copy, back_copy, fwd_copy, val_copy, wg_copy, ig_copy):
+    for hop in (0, 1, 3, 2):
+        ig_finish(hop)
+
+    for single in (in_copy, back_copy, fwd_copy, val_copy, wg_copy):
         single.wait_send()
 
     def drain(hop, carry):
-        for each in (ag_x, ag_y, ag_a, ag_b, rs_a, rs_b, rs_x, rs_y):
+        for each in (ag_x, ag_y, ag_a, ag_b, rs_a, rs_b, rs_x, rs_y, ig_copy):
             each(hop).wait_send()
         return carry
 
@@ -367,7 +394,6 @@
     ends = pltpu.VMEM((tiles, modes, LANES), F32)
     blocks = pltpu.VMEM((NZ, block, half), BF16)
     halves = pltpu.VMEM((NZ, mid, half), BF16)
-    mode_coef = mode_gain * jnp.sqrt(-jnp.expm1(-2.0 * decay_rate))
     in_grad, gate_grad, weight_grad = pl.pallas_call(
         functools.partial(chip_kernel, scale),
         out_shape=(
@@ -395,7 +421,7 @@
         compiler_params=pltpu.CompilerParams(
             collective_id=0, has_side_effects=True, vmem_limit_bytes=56 * 1024 * 1024
         ),
-    )(inputs[0], values[0], gating[0], out_grad[0], weight, decay_rate, mode_coef)
+    )(inputs[0], values[0], gating[0], out_grad[0], weight, decay_rate, mode_gain)
     return (in_grad[None], gate_grad[None], weight_grad)
 
 

time: 92.1 us -> 87.6 us (0.951)
  Pallas kernels: 84.5 us -> 81.8 us
  other arithmetic: 1.71 us -> 0 us
    pallas_call x1, Pallas kernels: 84.5 us -> 81.8 us  [on_chip_grid(): pl.pallas_call(functools.partial(chip_kernel, scale), out_shape=(jax.Shap...]
    mul x1 -> x0, other arithmetic: 1.71 us -> none  [on_chip_grid(): mode_coef = mode_gain * jnp.sqrt(-jnp.expm1(-2.0 * decay_rate))]
where the time goes in v2:
time: 87.6 us; the launch traced here: 87.4 us
  Pallas kernels  81.8 us (93%)
  local copies, waits for them, and re-layouts  4.96 us (6%)
    pallas_call x1, Pallas kernels, on_chip_grid(): pl.pallas_call(functools.partial(chip_kernel, scale), out_shape=(jax.Shap...  81.8 us
    unnamed x7, local copies, waits for them, and re-layouts  4.96 us

profile of v2, /device:TPU:1, one launch (start us, length us, event | category | flops | bytes accessed | tf_op | source)
XLA Modules:
  0.0 87.4 jit_solution(16873965604954567133)
XLA Ops:
  0.6 81.8 %shard_map.94 = (f32[128,2048]{1,0:T(8,128)}, f32[128,2048]{1,0:T(8,128)}, f32[128,2048]{1,0:T(8,128)}) custom-call(bf16[128,2048]{1,0:T(8,128)(2,1)} %bitcast.8, bf16[128,2048]{1,0:T(8,128)(2,1)} %bitcast.9, bf16[128,2048]{1,0:T(8,128)(2,1)} %bitcast.10, bf16[128,2048]{1,0:T(8,128)(2,1)} %bitcast.11, bf16[128,2048]{1,0:T(8,128)(2,1)} %weight_ref.1, ...), custom_call_target="tpu_custom_call" | custom-call | tf_op jit(solution)/shard_map/pallas_call | solution.py:397
  82.4 0.0 copy-start.1
  82.4 2.4 %copy.13 = f32[1,128,2048]{2,1,0:T(8,128)} copy(f32[1,128,2048]{2,1,0:T(8,128)} %bitcast.7) | data formatting | bytes 2097152
  84.8 0.0 copy-done.1
  84.8 0.0 copy-start
  84.8 1.0 %copy.14 = f32[1,128,2048]{2,1,0:T(8,128)} copy(f32[1,128,2048]{2,1,0:T(8,128)S(1)} %bitcast.6) | data formatting | bytes 2097152
  85.8 0.6 copy-done
  86.4 1.0 %copy.15 = f32[128,2048]{1,0:T(8,128)} copy(f32[128,2048]{1,0:T(8,128)S(1)} %copy-done) | data formatting | bytes 2097152
Async XLA Ops:
  82.4 2.4 %copy-start.1 = (f32[128,2048]{1,0:T(8,128)S(1)}, f32[128,2048]{1,0:T(8,128)}, u32[]{:S(2)}) copy-start(f32[128,2048]{1,0:T(8,128)} %get-tuple-element.7) | copy-start | bytes 3145732
  84.8 1.6 %copy-start = (f32[128,2048]{1,0:T(8,128)S(1)}, f32[128,2048]{1,0:T(8,128)}, u32[]{:S(2)}) copy-start(f32[128,2048]{1,0:T(8,128)} %get-tuple-element.14) | copy-start | bytes 3145732

commit v3 on v2

--- a/solution.py
+++ b/solution.py
@@ -65,28 +65,44 @@
     return decay, lam, coef
 
 
+def in_order(reverse):
+    return range(RUN - 1, -1, -1) if reverse else range(RUN)
+
+
 def run_states(series, decay, lam, states, ends, tile, reverse):
-    order = range(RUN - 1, -1, -1) if reverse else range(RUN)
-    steps = [series[tile, run_rows(step), :] for step in order]
+    modes = range(decay.shape[0])
+    rates = [spread(lam[mode : mode + 1]) for mode in modes]
+    held = None
+    for step in in_order(reverse):
+        column = series[tile, run_rows(step), :]
+        held = [column] * len(rates) if held is None else [r * h + column for r, h in zip(rates, held)]
     over_run = jnp.exp(-float(RUN) * decay)
-    for mode in range(decay.shape[0]):
-        rate = spread(lam[mode : mode + 1])
-        state = steps[0]
-        for column in steps[1:]:
-            state = rate * state + column
-        span = spread(over_run[mode : mode + 1])
-        for by in (1, 2, 4):
-            state = state + span * shifted_runs(state, by, reverse)
-            span = span * span
-        states[tile, mode] = state
-        last = 0 if reverse else RUNS - 1
-        ends[tile, mode : mode + 1, :] = state[last : last + 1]
-
-
-def run_outputs(series, impulse, decay, lam, coef, states, incoming, enters, result, tile, reverse):
-    order = list(range(RUN - 1, -1, -1) if reverse else range(RUN))
+    spans = [spread(over_run[mode : mode + 1]) for mode in modes]
+    for by in (1, 2, 4):
+        held = [h + s * shifted_runs(h, by, reverse) for h, s in zip(held, spans)]
+        spans = [s * s for s in spans]
+    last = 0 if reverse else RUNS - 1
+    for mode in modes:
+        states[tile, mode] = held[mode]
+        ends[tile, mode : mode + 1, :] = held[mode][last : last + 1]
+
+
+def added(terms):
+    while len(terms) > 1:
+        odd = terms[-1:] if len(terms) % 2 else []
+        terms = [a + b for a, b in zip(terms[::2], terms[1::2])] + odd
+    return terms[0]
+
+
+def run_within(series, impulse, result, tile, reverse):
+    order = list(in_order(reverse))
     steps = [series[tile, run_rows(step), :] for step in order]
     lags = [spread(impulse[tile, lag : lag + 1, :]) for lag in range(RUN)]
+    for at, step in enumerate(order):
+        result[tile, run_rows(step), :] = added([lags[at - b] * steps[b] for b in range(at + 1)])
+
+
+def run_carried(decay, lam, coef, states, incoming, enters, result, tile, reverse):
     ahead = row_index()
     ahead = (RUNS - 1 - ahead if reverse else ahead).astype(F32) * float(RUN)
     rates, carried = [], []
@@ -97,12 +113,8 @@
         prior = prior + jnp.exp(-ahead * spread(decay[mode : mode + 1])) * entry
         rates.append(rate)
         carried.append(spread(coef[mode : mode + 1]) * rate * prior)
-    for at, step in enumerate(order):
-        terms = [lags[at - back] * steps[back] for back in range(at + 1)] + carried
-        while len(terms) > 1:
-            odd = terms[-1:] if len(terms) % 2 else []
-            terms = [a + b for a, b in zip(terms[::2], terms[1::2])] + odd
-        result[tile, run_rows(step), :] = terms[0]
+    for step in in_order(reverse):
+        result[tile, run_rows(step), :] += added(carried)
         carried = [rate * item for rate, item in zip(rates, carried)]
 
 
@@ -215,18 +227,17 @@
     back_copy = copy(ends_b, enter_b, BACK_COPY, sibling)
     back_copy.start()
     ag_z(3).start()
-    lax.fori_loop(0, tiles, fwd_states, 0)
-    fwd_copy = copy(ends_f, enter_f, FWD_COPY, sibling)
-    fwd_copy.start()
-    ag_second(1)
-    ag_third(0)
+
+    def back_within(tile, carry):
+        run_within(series_b, impulse, result, tile, True)
+        return carry
+
+    lax.fori_loop(0, tiles, back_within, 0)
     back_copy.wait_recv()
 
     def val_tile(tile):
         decay, lam, coef = modes_of(decay_ref, gain_ref, tile)
-        run_outputs(
-            series_b, impulse, decay, lam, coef, states_b, enter_b, core == 0, result, tile, True
-        )
+        run_carried(decay, lam, coef, states_b, enter_b, core == 0, result, tile, True)
         return result[tile].astype(BF16)
 
     def val_other(tile, carry):
@@ -240,6 +251,8 @@
     lax.fori_loop(0, half_tiles, val_other, 0)
     val_copy = copy(val_send, val_full.at[own_rows, :], VAL_COPY, sibling)
     val_copy.start()
+    ag_second(1)
+    ag_third(0)
     lax.fori_loop(0, half_tiles, val_own, 0)
     ag_z(2).start()
     in_copy.wait_recv()
@@ -284,23 +297,25 @@
     for hop in (1, 2, 3, 0):
         rs_first(hop)
     ag_second(3)
-
-    fwd_copy.wait_recv()
-
-    def gate_tile(tile, carry):
-        decay, lam, coef = modes_of(decay_ref, gain_ref, tile)
-        run_outputs(
-            series_f, impulse, decay, lam, coef, states_f, enter_f, core == 1, result, tile, False
-        )
-        lanes = lanes_of(tile)
-        gate_ref[:, lanes] = grad_ref[:, lanes].astype(F32) * result[tile]
-        return carry
-
-    lax.fori_loop(0, tiles, gate_tile, 0)
+    lax.fori_loop(0, tiles, fwd_states, 0)
+    fwd_copy = copy(ends_f, enter_f, FWD_COPY, sibling)
+    fwd_copy.start()
 
     for hop in (1, 2, 3, 0):
         rs_second(hop)
     ag_second(2)
+
+    fwd_copy.wait_recv()
+
+    def gate_tile(tile, carry):
+        decay, lam, coef = modes_of(decay_ref, gain_ref, tile)
+        run_within(series_f, impulse, result, tile, False)
+        run_carried(decay, lam, coef, states_f, enter_f, core == 1, result, tile, False)
+        lanes = lanes_of(tile)
+        gate_ref[:, lanes] = grad_ref[:, lanes].astype(F32) * result[tile]
+        return carry
+
+    lax.fori_loop(0, tiles, gate_tile, 0)
 
     def own_sum(hop):
         total = term(chip((z + hop) % NZ, y, x))

time: 87.6 us -> 87.6 us (level)
  no operation moved by 1% of the time
where the time goes in v3:
time: 87.6 us; the launch traced here: 87.4 us
  Pallas kernels  81.8 us (93%)
  local copies, waits for them, and re-layouts  4.96 us (6%)
    pallas_call x1, Pallas kernels, on_chip_grid(): pl.pallas_call(functools.partial(chip_kernel, scale), out_shape=(jax.Shap...  81.8 us
    unnamed x7, local copies, waits for them, and re-layouts  4.96 us

profile of v3, /device:TPU:1, one launch (start us, length us, event | category | flops | bytes accessed | tf_op | source)
XLA Modules:
  0.0 87.4 jit_solution(5592201649958987501)
XLA Ops:
  0.6 81.8 %shard_map.94 = (f32[128,2048]{1,0:T(8,128)}, f32[128,2048]{1,0:T(8,128)}, f32[128,2048]{1,0:T(8,128)}) custom-call(bf16[128,2048]{1,0:T(8,128)(2,1)} %bitcast.8, bf16[128,2048]{1,0:T(8,128)(2,1)} %bitcast.9, bf16[128,2048]{1,0:T(8,128)(2,1)} %bitcast.10, bf16[128,2048]{1,0:T(8,128)(2,1)} %bitcast.11, bf16[128,2048]{1,0:T(8,128)(2,1)} %weight_ref.1, ...), custom_call_target="tpu_custom_call" | custom-call | tf_op jit(solution)/shard_map/pallas_call | solution.py:412
  82.4 0.0 copy-start.1
  82.4 2.4 %copy.13 = f32[1,128,2048]{2,1,0:T(8,128)} copy(f32[1,128,2048]{2,1,0:T(8,128)} %bitcast.7) | data formatting | bytes 2097152
  84.8 0.0 copy-done.1
  84.8 0.0 copy-start
  84.8 1.0 %copy.14 = f32[1,128,2048]{2,1,0:T(8,128)} copy(f32[1,128,2048]{2,1,0:T(8,128)S(1)} %bitcast.6) | data formatting | bytes 2097152
  85.8 0.6 copy-done
  86.4 1.0 %copy.15 = f32[128,2048]{1,0:T(8,128)} copy(f32[128,2048]{1,0:T(8,128)S(1)} %copy-done) | data formatting | bytes 2097152
Async XLA Ops:
  82.4 2.4 %copy-start.1 = (f32[128,2048]{1,0:T(8,128)S(1)}, f32[128,2048]{1,0:T(8,128)}, u32[]{:S(2)}) copy-start(f32[128,2048]{1,0:T(8,128)} %get-tuple-element.7) | copy-start | bytes 3145732
  84.8 1.6 %copy-start = (f32[128,2048]{1,0:T(8,128)S(1)}, f32[128,2048]{1,0:T(8,128)}, u32[]{:S(2)}) copy-start(f32[128,2048]{1,0:T(8,128)} %get-tuple-element.14) | copy-start | bytes 3145732

commit v4 on v3

--- a/solution.py
+++ b/solution.py
@@ -18,8 +18,8 @@
 NZ = 4
 
 IN_COPY, BACK_COPY, FWD_COPY, VAL_COPY, WG_COPY = range(5)
-AG_Z, AG_X, AG_Y, AG_A, AG_B, RS_A, RS_B, RS_X, RS_Y, RS_Z, IG_COPY = range(5, 49, 4)
-COPIES = 49
+AG_Z, AG_X, AG_Y, AG_A, AG_B, RS_A, RS_B, RS_X, RS_Y, RS_Z, IG_COPY, AG_P = range(5, 53, 4)
+COPIES = 53
 
 
 def dot(lhs, rhs, lhs_dim, rhs_dim):
@@ -120,14 +120,14 @@
 
 def chip_kernel(
     scale,
-    in_ref, values_ref, gating_ref, grad_ref, weight_ref, decay_ref, gain_ref,
+    in_hbm, values_hbm, gating_hbm, grad_hbm, weight_hbm, decay_ref, gain_ref,
     ig_ref, gate_ref, wg_ref,
-    series_f, series_b, result, impulse, states_f, states_b,
+    values_ref, gating_ref, grad_ref, series_f, series_b, result, impulse, states_f, states_b,
     ends_f, ends_b, enter_f, enter_b,
     in_full, val_full, val_send, wfull,
     s1, r1a, r1b, s2x, s2y, r2x, r2y, s3, r3,
     ig_send, ig_recv, wg_send, wg_recv,
-    send_sem, recv_sem,
+    send_sem, recv_sem, load_sem,
 ):
     core = lax.axis_index("ctx")
     dp = lax.axis_index("dp")
@@ -135,8 +135,9 @@
     tiles = series_f.shape[0]
     half_tiles = tiles // 2
     half = half_tiles * LANES
-    block = weight_ref.shape[0]
+    block = weight_hbm.shape[0]
     mid = block // 2
+    cut = block // 4
 
     def chip(cz, cy, cx):
         return cz * 4 + cy * 2 + cx
@@ -154,6 +155,21 @@
             device_id=device, device_id_type=MESH,
         )
 
+    own_half = pl.ds(pl.multiple_of(core * half, half), half)
+    other_half = pl.ds(pl.multiple_of((1 - core) * half, half), half)
+    own_rows = pl.ds(pl.multiple_of(core * ROWS, ROWS), ROWS)
+
+    def load(src, dst, which):
+        return pltpu.make_async_copy(src, dst, load_sem.at[which])
+
+    weight_load = load(weight_hbm.at[:, own_half], wfull.at[dp], 0)
+    gating_load = load(gating_hbm, gating_ref, 1)
+    grad_load = load(grad_hbm, grad_ref, 2)
+    in_load = load(in_hbm, in_full.at[own_rows, :], 3)
+    values_load = load(values_hbm, values_ref, 4)
+    for each in (weight_load, gating_load, grad_load, in_load, values_load):
+        each.start()
+
     barrier = pltpu.get_barrier_semaphore()
     partners = [sibling, x_dev, y_dev] + [z_dev(hop) for hop in range(1, NZ)]
     for device in partners:
@@ -161,31 +177,48 @@
     pl.semaphore_wait(barrier, len(partners))
 
     def wrows(index, start=0, size=block):
-        return wfull.at[pl.ds(pl.multiple_of(index * block + start, mid), size), :]
-
-    own_half = pl.ds(pl.multiple_of(core * half, half), half)
-    other_half = pl.ds(pl.multiple_of((1 - core) * half, half), half)
-    own_rows = pl.ds(pl.multiple_of(core * ROWS, ROWS), ROWS)
-
-    wrows(dp)[...] = weight_ref[:, own_half]
+        return wfull.at[index, pl.ds(start, size), :]
+
+    weight_load.wait()
+
+    def from_hop(hop):
+        return (z - hop + NZ) % NZ
 
     def ag_z(hop):
-        return copy(wrows(dp), wrows(dp), AG_Z + hop, z_dev(hop))
+        rows = wrows(dp, cut, block - cut)
+        return copy(rows, rows, AG_Z + hop, z_dev(hop))
+
+    def ag_p(hop):
+        rows = wfull.at[pl.ds(z * 4, 4), pl.ds(0, cut), :]
+        return copy(rows, rows, AG_P + hop, z_dev(hop))
+
+    def whole(hop, cy, cx):
+        index = chip(from_hop(hop), cy, cx)
+        return wrows(index, cut, block - cut) if hop else wrows(index)
+
+    def first_part(hop, cy, cx):
+        index = chip(from_hop(hop), cy, cx)
+        return wrows(index, cut, (block - cut) // 2) if hop else wrows(index, 0, mid)
+
+    def second_part(hop, cy, cx):
+        index = chip(from_hop(hop), cy, cx)
+        size = (block - cut) // 2 if hop else mid
+        return wrows(index, block - size, size)
 
     def ag_x(hop):
-        rows = wrows(chip((z - hop + NZ) % NZ, y, x))
+        rows = whole(hop, y, x)
         return copy(rows, rows, AG_X + hop, x_dev)
 
     def ag_y(hop):
-        rows = wrows(chip((z - hop + NZ) % NZ, y, x))
+        rows = whole(hop, y, x)
         return copy(rows, rows, AG_Y + hop, y_dev)
 
     def ag_a(hop):
-        rows = wrows(chip((z - hop + NZ) % NZ, y, 1 - x), 0, mid)
+        rows = first_part(hop, y, 1 - x)
         return copy(rows, rows, AG_A + hop, y_dev)
 
     def ag_b(hop):
-        rows = wrows(chip((z - hop + NZ) % NZ, 1 - y, x), mid, mid)
+        rows = second_part(hop, 1 - y, x)
         return copy(rows, rows, AG_B + hop, x_dev)
 
     def ag_second(hop):
@@ -202,9 +235,10 @@
     ag_z(1).start()
     ag_x(0).start()
     ag_y(0).start()
-    in_copy = copy(in_ref, in_full.at[own_rows, :], IN_COPY, sibling)
+    in_copy = copy(in_hbm, in_full.at[own_rows, :], IN_COPY, sibling)
     in_copy.start()
-    in_full[own_rows, :] = in_ref[...]
+    gating_load.wait()
+    grad_load.wait()
 
     def back_states(tile, carry):
         lanes = lanes_of(tile)
@@ -255,6 +289,7 @@
     ag_third(0)
     lax.fori_loop(0, half_tiles, val_own, 0)
     ag_z(2).start()
+    in_load.wait()
     in_copy.wait_recv()
     val_copy.wait_recv()
 
@@ -297,6 +332,10 @@
     for hop in (1, 2, 3, 0):
         rs_first(hop)
     ag_second(3)
+    ag_a(0).wait_recv()
+    for hop in (1, 3, 2):
+        ag_p(hop).start()
+    values_load.wait()
     lax.fori_loop(0, tiles, fwd_states, 0)
     fwd_copy = copy(ends_f, enter_f, FWD_COPY, sibling)
     fwd_copy.start()
@@ -345,11 +384,15 @@
 
     def ig_part(hop):
         cz = (z - hop + NZ) % NZ
-        ag_a(hop).wait_recv()
+        if hop:
+            ag_a(hop).wait_recv()
+            ag_p(hop).wait_recv()
         ag_b(hop).wait_recv()
         for cy in range(2):
-            first = pl.multiple_of(chip(cz, cy, 0) * block, 2 * block)
-            part = dot(val_full[...], wfull[pl.ds(first, 2 * block), :], 1, 1)
+            pair = chip(cz, cy, 0)
+            first = pl.multiple_of(pair * block, 2 * block)
+            rows = wfull[pl.ds(pair, 2)].reshape(2 * block, half)
+            part = dot(val_full[...], rows, 1, 1)
             columns = pl.ds(first, 2 * block)
             top, bottom = part[:ROWS], part[ROWS:]
             ig_ref[:, columns] = jnp.where(core == 0, top, bottom)
@@ -382,18 +425,12 @@
     for single in (in_copy, back_copy, fwd_copy, val_copy, wg_copy):
         single.wait_send()
 
-    def drain(hop, carry):
+    for hop in range(NZ):
         for each in (ag_x, ag_y, ag_a, ag_b, rs_a, rs_b, rs_x, rs_y, ig_copy):
             each(hop).wait_send()
-        return carry
-
-    def drain_z(hop, carry):
-        ag_z(hop).wait_send()
-        rs_z(hop).wait_send()
-        return carry
-
-    lax.fori_loop(0, NZ, drain, 0)
-    lax.fori_loop(1, NZ, drain_z, 0)
+        if hop:
+            for each in (ag_z, ag_p, rs_z):
+                each(hop).wait_send()
 
 
 def on_chip_grid(inputs, values, gating, out_grad, weight, decay_rate, mode_gain):
@@ -416,15 +453,18 @@
             jax.ShapeDtypeStruct((rows, channels), F32),
             jax.ShapeDtypeStruct((block, channels), F32),
         ),
-        in_specs=[vmem] * 7,
+        in_specs=[pl.BlockSpec(memory_space=pl.ANY)] * 5 + [vmem] * 2,
         out_specs=(vmem,) * 3,
         scratch_shapes=[
+            pltpu.VMEM((rows, channels), BF16),
+            pltpu.VMEM((rows, channels), BF16),
+            pltpu.VMEM((rows, channels), BF16),
             series, series, series, pltpu.VMEM((tiles, RUN, LANES), F32), states, states,
             ends, ends, ends, ends,
             pltpu.VMEM((2 * rows, width), BF16),
             pltpu.VMEM((2 * rows, half), BF16),
             pltpu.VMEM((rows, half), BF16),
-            pltpu.VMEM((width, half), BF16),
+            pltpu.VMEM((width // block, block, half), BF16),
             blocks, halves, halves, blocks, blocks, blocks, blocks, blocks, blocks,
             pltpu.VMEM((rows, width), F32),
             pltpu.VMEM((rows, width), F32),
@@ -432,6 +472,7 @@
             pltpu.VMEM((block, half), F32),
             pltpu.SemaphoreType.DMA((COPIES,)),
             pltpu.SemaphoreType.DMA((COPIES,)),
+            pltpu.SemaphoreType.DMA((5,)),
         ],
         compiler_params=pltpu.CompilerParams(
             collective_id=0, has_side_effects=True, vmem_limit_bytes=56 * 1024 * 1024

time: 87.6 us -> 79.3 us (0.905)
  Pallas kernels: 81.8 us -> 73.5 us
    pallas_call x1, Pallas kernels: 81.8 us -> 73.5 us  [on_chip_grid(): pl.pallas_call(functools.partial(chip_kernel, scale), out_shape=(jax.Shap...]
where the time goes in v4:
time: 79.3 us; the launch traced here: 79.1 us
  Pallas kernels  73.5 us (93%)
  local copies, waits for them, and re-layouts  4.96 us (6%)
    pallas_call x1, Pallas kernels, on_chip_grid(): pl.pallas_call(functools.partial(chip_kernel, scale), out_shape=(jax.Shap...  73.5 us
    unnamed x7, local copies, waits for them, and re-layouts  4.96 us

profile of v4, /device:TPU:1, one launch (start us, length us, event | category | flops | bytes accessed | tf_op | source)
XLA Modules:
  0.0 79.1 jit_solution(14579263572867954566)
XLA Ops:
  0.6 73.5 %shard_map.94 = (f32[128,2048]{1,0:T(8,128)}, f32[128,2048]{1,0:T(8,128)}, f32[128,2048]{1,0:T(8,128)}) custom-call(bf16[128,2048]{1,0:T(8,128)(2,1)} %bitcast.8, bf16[128,2048]{1,0:T(8,128)(2,1)} %bitcast.9, bf16[128,2048]{1,0:T(8,128)(2,1)} %bitcast.10, bf16[128,2048]{1,0:T(8,128)(2,1)} %bitcast.11, bf16[128,2048]{1,0:T(8,128)(2,1)} %weight_hbm.1, ...), custom_call_target="tpu_custom_call" | custom-call | tf_op jit(solution)/shard_map/pallas_call | solution.py:449
  74.1 0.0 copy-start.1
  74.1 2.4 %copy.13 = f32[1,128,2048]{2,1,0:T(8,128)} copy(f32[1,128,2048]{2,1,0:T(8,128)} %bitcast.7) | data formatting | bytes 2097152
  76.5 0.0 copy-done.1
  76.5 0.0 copy-start
  76.5 1.0 %copy.14 = f32[1,128,2048]{2,1,0:T(8,128)} copy(f32[1,128,2048]{2,1,0:T(8,128)S(1)} %bitcast.6) | data formatting | bytes 2097152
  77.5 0.6 copy-done
  78.1 1.0 %copy.15 = f32[128,2048]{1,0:T(8,128)} copy(f32[128,2048]{1,0:T(8,128)S(1)} %copy-done) | data formatting | bytes 2097152
Async XLA Ops:
  74.1 2.4 %copy-start.1 = (f32[128,2048]{1,0:T(8,128)S(1)}, f32[128,2048]{1,0:T(8,128)}, u32[]{:S(2)}) copy-start(f32[128,2048]{1,0:T(8,128)} %get-tuple-element.7) | copy-start | bytes 3145732
  76.5 1.6 %copy-start = (f32[128,2048]{1,0:T(8,128)S(1)}, f32[128,2048]{1,0:T(8,128)}, u32[]{:S(2)}) copy-start(f32[128,2048]{1,0:T(8,128)} %get-tuple-element.14) | copy-start | bytes 3145732

commit v5 on v4

--- a/solution.py
+++ b/solution.py
@@ -267,6 +267,8 @@
         return carry
 
     lax.fori_loop(0, tiles, back_within, 0)
+    ag_z(2).start()
+    ag_third(0)
     back_copy.wait_recv()
 
     def val_tile(tile):
@@ -286,9 +288,7 @@
     val_copy = copy(val_send, val_full.at[own_rows, :], VAL_COPY, sibling)
     val_copy.start()
     ag_second(1)
-    ag_third(0)
     lax.fori_loop(0, half_tiles, val_own, 0)
-    ag_z(2).start()
     in_load.wait()
     in_copy.wait_recv()
     val_copy.wait_recv()
@@ -329,12 +329,13 @@
         s2y[hop, pl.ds(mid, mid), :] = (to_y[mid:] + r1b[hop].astype(F32)).astype(BF16)
         rs_y(hop).start()
 
-    for hop in (1, 2, 3, 0):
-        rs_first(hop)
-    ag_second(3)
+    rs_first(1)
     ag_a(0).wait_recv()
     for hop in (1, 3, 2):
         ag_p(hop).start()
+    for hop in (2, 3, 0):
+        rs_first(hop)
+    ag_second(3)
     values_load.wait()
     lax.fori_loop(0, tiles, fwd_states, 0)
     fwd_copy = copy(ends_f, enter_f, FWD_COPY, sibling)
@@ -431,6 +432,34 @@
         if hop:
             for each in (ag_z, ag_p, rs_z):
                 each(hop).wait_send()
+
+
+def write_kernel(ig_ref, gate_ref, wg_ref, ig_out, gate_out, wg_out):
+    ig_out[0] = ig_ref[...]
+    gate_out[0] = gate_ref[...]
+    wg_out[...] = wg_ref[...]
+
+
+def written(in_grad, gate_grad, weight_grad):
+    steps = 4
+    flat = [pl.BlockSpec((a.shape[0] // steps, a.shape[1]), lambda i: (i, 0)) for a in (in_grad, gate_grad, weight_grad)]
+    rows, width = in_grad.shape
+    channels = gate_grad.shape[1]
+    return pl.pallas_call(
+        write_kernel,
+        grid=(steps,),
+        out_shape=(
+            jax.ShapeDtypeStruct((1, rows, width), F32),
+            jax.ShapeDtypeStruct((1, rows, channels), F32),
+            jax.ShapeDtypeStruct(weight_grad.shape, F32),
+        ),
+        in_specs=flat,
+        out_specs=(
+            pl.BlockSpec((1, rows // steps, width), lambda i: (0, i, 0)),
+            pl.BlockSpec((1, rows // steps, channels), lambda i: (0, i, 0)),
+            flat[2],
+        ),
+    )(in_grad, gate_grad, weight_grad)
 
 
 def on_chip_grid(inputs, values, gating, out_grad, weight, decay_rate, mode_gain):
@@ -478,7 +507,7 @@
             collective_id=0, has_side_effects=True, vmem_limit_bytes=56 * 1024 * 1024
         ),
     )(inputs[0], values[0], gating[0], out_grad[0], weight, decay_rate, mode_gain)
-    return (in_grad[None], gate_grad[None], weight_grad)
+    return written(in_grad, gate_grad, weight_grad)
 
 
 def fits_chip_grid(mesh):

time: 79.3 us -> 79.7 us (level)
  Pallas kernels: 73.5 us -> 78.9 us
  local copies, waits for them, and re-layouts: 4.96 us -> 0 us
    unnamed x7 -> x0, local copies, waits for them, and re-layouts: 4.96 us -> none
    pallas_call x0 -> x1, Pallas kernels: none -> 4.14 us  [written(): pl.pallas_call(write_kernel, grid=(steps,), out_shape=(jax.ShapeDtypeStru...]
    pallas_call x1, Pallas kernels: 73.5 us -> 74.8 us  [on_chip_grid(): pl.pallas_call(functools.partial(chip_kernel, scale), out_shape=(jax.Shap...]
where the time goes in v5:
time: 79.7 us; the launch traced here: 79.5 us
  Pallas kernels  78.9 us (99%)
    pallas_call x1, Pallas kernels, on_chip_grid(): pl.pallas_call(functools.partial(chip_kernel, scale), out_shape=(jax.Shap...  74.8 us
    pallas_call x1, Pallas kernels, written(): pl.pallas_call(write_kernel, grid=(steps,), out_shape=(jax.ShapeDtypeStru...  4.14 us

profile of v5, /device:TPU:1, one launch (start us, length us, event | category | flops | bytes accessed | tf_op | source)
XLA Modules:
  0.0 79.5 jit_solution(17705271002473455804)
XLA Ops:
  0.6 74.8 %shard_map.94 = (f32[128,2048]{1,0:T(8,128)}, f32[128,2048]{1,0:T(8,128)}, f32[128,2048]{1,0:T(8,128)}) custom-call(bf16[128,2048]{1,0:T(8,128)(2,1)} %bitcast.4, bf16[128,2048]{1,0:T(8,128)(2,1)} %bitcast.5, bf16[128,2048]{1,0:T(8,128)(2,1)} %bitcast.6, bf16[128,2048]{1,0:T(8,128)(2,1)} %bitcast.7, bf16[128,2048]{1,0:T(8,128)(2,1)} %weight_hbm.1, ...), custom_call_target="tpu_custom_call" | custom-call | tf_op jit(solution)/shard_map/pallas_call | solution.py:478
  75.4 4.1 %shard_map.95 = (f32[1,128,2048]{2,1,0:T(8,128)}, f32[1,128,2048]{2,1,0:T(8,128)}, f32[128,2048]{1,0:T(8,128)}) custom-call(f32[128,2048]{1,0:T(8,128)} %get-tuple-element.6.ig_ref, f32[128,2048]{1,0:T(8,128)} %get-tuple-element.7.gate_ref, f32[128,2048]{1,0:T(8,128)} %get-tuple-element.8.wg_ref), custom_call_target="tpu_custom_call" | custom-call | tf_op jit(solution)/shard_map/pallas_call | solution.py:448

commit v6 on v4

--- a/solution.py
+++ b/solution.py
@@ -19,13 +19,18 @@
 
 IN_COPY, BACK_COPY, FWD_COPY, VAL_COPY, WG_COPY = range(5)
 AG_Z, AG_X, AG_Y, AG_A, AG_B, RS_A, RS_B, RS_X, RS_Y, RS_Z, IG_COPY, AG_P = range(5, 53, 4)
-COPIES = 53
+AG_ZF, AG_PF, COPIES = range(53, 56)
+WRITES = 4
 
 
 def dot(lhs, rhs, lhs_dim, rhs_dim):
     return lax.dot_general(
         lhs, rhs, (((lhs_dim,), (rhs_dim,)), ((), ())), preferred_element_type=F32
     )
+
+
+def own_plane(hop):
+    return isinstance(hop, int) and hop == 0
 
 
 def lanes_of(tile):
@@ -137,7 +142,7 @@
     half = half_tiles * LANES
     block = weight_hbm.shape[0]
     mid = block // 2
-    cut = block // 4
+    cut = 3 * block // 8
 
     def chip(cz, cy, cx):
         return cz * 4 + cy * 2 + cx
@@ -149,9 +154,10 @@
     def z_dev(hop):
         return (core, chip((z + hop) % NZ, y, x))
 
-    def copy(src, dst, which, device):
+    def copy(src, dst, which, device, into=None):
+        into = which if into is None else into
         return pltpu.make_async_remote_copy(
-            src_ref=src, dst_ref=dst, send_sem=send_sem.at[which], recv_sem=recv_sem.at[which],
+            src_ref=src, dst_ref=dst, send_sem=send_sem.at[which], recv_sem=recv_sem.at[into],
             device_id=device, device_id_type=MESH,
         )
 
@@ -181,29 +187,57 @@
 
     weight_load.wait()
 
+    edge = (z == 0) | (z == NZ - 1)
+    near = jnp.where(z == 0, 3, 1)
+    second = jnp.where(edge, 2, 3)
+    last = jnp.where(z == 0, 1, jnp.where(z == NZ - 1, 3, 2))
+
     def from_hop(hop):
         return (z - hop + NZ) % NZ
 
+    def z_rows():
+        return wrows(dp, cut, block - cut)
+
+    def p_rows(cz):
+        return wfull.at[pl.ds(cz * 4, 4), pl.ds(0, cut), :]
+
     def ag_z(hop):
-        rows = wrows(dp, cut, block - cut)
-        return copy(rows, rows, AG_Z + hop, z_dev(hop))
+        return copy(z_rows(), z_rows(), AG_Z + hop, z_dev(hop))
 
     def ag_p(hop):
-        rows = wfull.at[pl.ds(z * 4, 4), pl.ds(0, cut), :]
-        return copy(rows, rows, AG_P + hop, z_dev(hop))
+        return copy(p_rows(z), p_rows(z), AG_P + hop, z_dev(hop))
+
+    beside = (core, chip(jnp.where(z == 2, 3, 0), y, x))
+    beside_hop = jnp.where(z == 2, 3, 1)
+
+    def ag_zf():
+        rows = wrows(chip(from_hop(2), y, x), cut, block - cut)
+        return copy(rows, rows, AG_ZF, beside, AG_Z + beside_hop)
+
+    def ag_pf():
+        rows = p_rows(from_hop(2))
+        return copy(rows, rows, AG_PF, beside, AG_P + beside_hop)
+
+    def if_direct(hop, act):
+        if hop == 2:
+            act()
+        else:
+            pl.when(z != (NZ - 1 if hop == 1 else 0))(act)
+
+    mid_cut = 3 * block // 4
 
     def whole(hop, cy, cx):
         index = chip(from_hop(hop), cy, cx)
-        return wrows(index, cut, block - cut) if hop else wrows(index)
+        return wrows(index) if own_plane(hop) else wrows(index, cut, block - cut)
 
     def first_part(hop, cy, cx):
         index = chip(from_hop(hop), cy, cx)
-        return wrows(index, cut, (block - cut) // 2) if hop else wrows(index, 0, mid)
+        return wrows(index, 0, cut) if own_plane(hop) else wrows(index, cut, mid_cut - cut)
 
     def second_part(hop, cy, cx):
         index = chip(from_hop(hop), cy, cx)
-        size = (block - cut) // 2 if hop else mid
-        return wrows(index, block - size, size)
+        start = cut if own_plane(hop) else mid_cut
+        return wrows(index, start, block - start)
 
     def ag_x(hop):
         rows = whole(hop, y, x)
@@ -232,7 +266,8 @@
         ag_y(hop).wait_recv()
         ag_b(hop).start()
 
-    ag_z(1).start()
+    if_direct(1, lambda: ag_z(1).start())
+    if_direct(3, lambda: ag_z(3).start())
     ag_x(0).start()
     ag_y(0).start()
     in_copy = copy(in_hbm, in_full.at[own_rows, :], IN_COPY, sibling)
@@ -260,13 +295,15 @@
     lax.fori_loop(0, tiles, back_states, 0)
     back_copy = copy(ends_b, enter_b, BACK_COPY, sibling)
     back_copy.start()
-    ag_z(3).start()
+    ag_z(2).start()
 
     def back_within(tile, carry):
         run_within(series_b, impulse, result, tile, True)
         return carry
 
     lax.fori_loop(0, tiles, back_within, 0)
+    ag_third(0)
+    ag_second(near)
     back_copy.wait_recv()
 
     def val_tile(tile):
@@ -285,10 +322,8 @@
     lax.fori_loop(0, half_tiles, val_other, 0)
     val_copy = copy(val_send, val_full.at[own_rows, :], VAL_COPY, sibling)
     val_copy.start()
-    ag_second(1)
-    ag_third(0)
+    ag_second(second)
     lax.fori_loop(0, half_tiles, val_own, 0)
-    ag_z(2).start()
     in_load.wait()
     in_copy.wait_recv()
     val_copy.wait_recv()
@@ -329,12 +364,19 @@
         s2y[hop, pl.ds(mid, mid), :] = (to_y[mid:] + r1b[hop].astype(F32)).astype(BF16)
         rs_y(hop).start()
 
-    for hop in (1, 2, 3, 0):
+    rs_first(1)
+    ag_a(0).wait_recv()
+    if_direct(1, lambda: ag_p(1).start())
+    if_direct(3, lambda: ag_p(3).start())
+    ag_p(2).start()
+    for hop in (2, 3, 0):
         rs_first(hop)
-    ag_second(3)
-    ag_a(0).wait_recv()
-    for hop in (1, 3, 2):
-        ag_p(hop).start()
+
+    @pl.when(jnp.logical_not(edge))
+    def _():
+        ag_second(2)
+        ag_zf().start()
+
     values_load.wait()
     lax.fori_loop(0, tiles, fwd_states, 0)
     fwd_copy = copy(ends_f, enter_f, FWD_COPY, sibling)
@@ -342,7 +384,16 @@
 
     for hop in (1, 2, 3, 0):
         rs_second(hop)
-    ag_second(2)
+
+    @pl.when(edge)
+    def _():
+        ag_second(last)
+
+    @pl.when(jnp.logical_not(edge))
+    def _():
+        ag_p(2).wait_recv()
+        ag_pf().start()
+
 
     fwd_copy.wait_recv()
 
@@ -367,12 +418,12 @@
         rs_z(hop).start()
 
     rs_third(1)
-    ag_third(1)
+    ag_third(near)
     rs_third(2)
-    ag_third(3)
+    ag_third(second)
     rs_third(3)
     wg_send[...] = own_sum(0)
-    ag_third(2)
+    ag_third(last)
 
     def ig_columns(hop):
         first = ((z - hop + NZ) % NZ) * 4 * block
@@ -384,9 +435,9 @@
 
     def ig_part(hop):
         cz = (z - hop + NZ) % NZ
-        if hop:
+        if not own_plane(hop):
             ag_a(hop).wait_recv()
-            ag_p(hop).wait_recv()
+            pl.when(edge | (hop != 2))(lambda: ag_p(hop).wait_recv())
         ag_b(hop).wait_recv()
         for cy in range(2):
             pair = chip(cz, cy, 0)
@@ -405,8 +456,8 @@
         ig_ref[:, columns] += ig_recv[:, columns]
 
     ig_part(0)
-    ig_part(1)
-    ig_part(3)
+    ig_part(near)
+    ig_part(second)
 
     for hop in range(1, NZ):
         rs_z(hop).wait_recv()
@@ -416,10 +467,10 @@
     wg_copy.start()
     wg_ref[:, own_half] = wg_send[...]
 
-    ig_part(2)
+    ig_part(last)
     wg_copy.wait_recv()
     wg_ref[:, other_half] = wg_recv[...]
-    for hop in (0, 1, 3, 2):
+    for hop in (0, near, second, last):
         ig_finish(hop)
 
     for single in (in_copy, back_copy, fwd_copy, val_copy, wg_copy):
@@ -429,8 +480,44 @@
         for each in (ag_x, ag_y, ag_a, ag_b, rs_a, rs_b, rs_x, rs_y, ig_copy):
             each(hop).wait_send()
         if hop:
-            for each in (ag_z, ag_p, rs_z):
-                each(hop).wait_send()
+            rs_z(hop).wait_send()
+            if_direct(hop, lambda: ag_z(hop).wait_send())
+            if_direct(hop, lambda: ag_p(hop).wait_send())
+
+    @pl.when(jnp.logical_not(edge))
+    def _():
+        ag_zf().wait_send()
+        ag_pf().wait_send()
+
+
+def write_kernel(ig_ref, gate_ref, wg_ref, ig_out, gate_out, wg_out, sems):
+    pairs = ((ig_ref, ig_out.at[0]), (gate_ref, gate_out.at[0]), (wg_ref, wg_out))
+    moves = []
+    for which, (src, dst) in enumerate(pairs):
+        part = src.shape[0] // WRITES
+        for at in range(WRITES):
+            rows = pl.ds(at * part, part)
+            sem = sems.at[which * WRITES + at]
+            moves.append(pltpu.make_async_copy(src.at[rows, :], dst.at[rows, :], sem))
+    for move in moves:
+        move.start()
+    for move in moves:
+        move.wait()
+
+
+def written(in_grad, gate_grad, weight_grad):
+    anywhere = pl.BlockSpec(memory_space=pl.ANY)
+    return pl.pallas_call(
+        write_kernel,
+        out_shape=(
+            jax.ShapeDtypeStruct((1,) + in_grad.shape, F32),
+            jax.ShapeDtypeStruct((1,) + gate_grad.shape, F32),
+            jax.ShapeDtypeStruct(weight_grad.shape, F32),
+        ),
+        in_specs=[anywhere] * 3,
+        out_specs=(anywhere,) * 3,
+        scratch_shapes=[pltpu.SemaphoreType.DMA((3 * WRITES,))],
+    )(in_grad, gate_grad, weight_grad)
 
 
 def on_chip_grid(inputs, values, gating, out_grad, weight, decay_rate, mode_gain):
@@ -475,10 +562,10 @@
             pltpu.SemaphoreType.DMA((5,)),
         ],
         compiler_params=pltpu.CompilerParams(
-            collective_id=0, has_side_effects=True, vmem_limit_bytes=56 * 1024 * 1024
+            collective_id=0, has_side_effects=True, vmem_limit_bytes=40 * 1024 * 1024
         ),
     )(inputs[0], values[0], gating[0], out_grad[0], weight, decay_rate, mode_gain)
-    return (in_grad[None], gate_grad[None], weight_grad)
+    return written(in_grad, gate_grad, weight_grad)
 
 
 def fits_chip_grid(mesh):

time: 79.3 us -> 178 us (2.24)
  Pallas kernels: 73.5 us -> 167 us
  local copies, waits for them, and re-layouts: 4.96 us -> 9.98 us
    pallas_call x0 -> x1, Pallas kernels: none -> 96.5 us  [written(): pl.pallas_call(write_kernel, out_shape=(jax.ShapeDtypeStruct((1,) + in_gr...]
    unnamed x7 -> x20, local copies, waits for them, and re-layouts: 4.96 us -> 9.98 us
    pallas_call x1, Pallas kernels: 73.5 us -> 70.6 us  [on_chip_grid(): pl.pallas_call(functools.partial(chip_kernel, scale), out_shape=(jax.Shap...]
where the time goes in v6:
time: 178 us
  Pallas kernels  167 us (94%)
  local copies, waits for them, and re-layouts  9.98 us (6%)
    pallas_call x1, Pallas kernels, written(): pl.pallas_call(write_kernel, out_shape=(jax.ShapeDtypeStruct((1,) + in_gr...  96.5 us
    pallas_call x1, Pallas kernels, on_chip_grid(): pl.pallas_call(functools.partial(chip_kernel, scale), out_shape=(jax.Shap...  70.6 us
    unnamed x20, local copies, waits for them, and re-layouts  9.98 us

profile of v6, /device:TPU:1, one launch (start us, length us, event | category | flops | bytes accessed | tf_op | source)
XLA Modules:
  0.0 177.8 jit_solution(15731104708589712183)
XLA Ops:
  0.6 0.0 copy-start.3
  0.6 1.0 copy-done.3
  1.7 0.0 copy-start.4
  1.7 1.0 copy-done.4
  2.7 0.0 copy-start.5
  2.7 1.0 copy-done.5
  3.8 0.0 copy-start.6
  3.8 1.0 copy-done.6
  4.8 0.0 copy-start.7
  4.8 1.0 copy-done.7
  5.8 0.0 copy-start.8
  5.8 0.9 copy-done.8
  6.7 0.0 copy-start.9
  6.8 0.9 copy-done.9
  7.7 70.6 %shard_map.94 = (f32[128,2048]{1,0:T(8,128)S(1)}, f32[128,2048]{1,0:T(8,128)S(1)}, f32[128,2048]{1,0:T(8,128)S(1)}) custom-call(bf16[128,2048]{1,0:T(8,128)(2,1)S(1)} %bitcast.4, bf16[128,2048]{1,0:T(8,128)(2,1)S(1)} %bitcast.5, bf16[128,2048]{1,0:T(8,128)(2,1)S(1)} %bitcast.6, bf16[128,2048]{1,0:T(8,128)(2,1)S(1)} %bitcast.7, ...), custom_call_target="tpu_custom_call" | custom-call | tf_op jit(solution)/shard_map/pallas_call | solution.py:536
  78.3 0.0 copy-start
  78.3 1.0 copy-done
  79.3 0.0 copy-start.1
  79.3 1.0 copy-done.1
  80.3 0.0 copy-start.2
  80.3 1.0 copy-done.2
  81.3 96.5 %shard_map.95 = (f32[1,128,2048]{2,1,0:T(8,128)}, f32[1,128,2048]{2,1,0:T(8,128)}, f32[128,2048]{1,0:T(8,128)}) custom-call(f32[128,2048]{1,0:T(8,128)} %copy-done, f32[128,2048]{1,0:T(8,128)} %copy-done.1, f32[128,2048]{1,0:T(8,128)} %copy-done.2), custom_call_target="tpu_custom_call" | custom-call | tf_op jit(solution)/shard_map/pallas_call | solution.py:510
Async XLA Ops:
  0.6 1.0 copy-start.3
  1.7 1.0 copy-start.4
  2.7 1.0 copy-start.5
  3.8 1.0 copy-start.6
  4.8 1.0 copy-start.7
  5.8 0.9 copy-start.8
  6.7 0.9 copy-start.9
  78.3 1.0 copy-start
  79.3 1.0 copy-start.1
  80.3 1.0 copy-start.2

commit v7 on v6

--- a/solution.py
+++ b/solution.py
@@ -126,13 +126,13 @@
 def chip_kernel(
     scale,
     in_hbm, values_hbm, gating_hbm, grad_hbm, weight_hbm, decay_ref, gain_ref,
-    ig_ref, gate_ref, wg_ref,
-    values_ref, gating_ref, grad_ref, series_f, series_b, result, impulse, states_f, states_b,
+    ig_hbm, gate_hbm, wg_hbm,
+    ig_ref, gate_ref, wg_ref, values_ref, gating_ref, grad_ref, series_f, series_b, result, impulse, states_f, states_b,
     ends_f, ends_b, enter_f, enter_b,
     in_full, val_full, val_send, wfull,
     s1, r1a, r1b, s2x, s2y, r2x, r2y, s3, r3,
     ig_send, ig_recv, wg_send, wg_recv,
-    send_sem, recv_sem, load_sem,
+    send_sem, recv_sem, load_sem, store_sem,
 ):
     core = lax.axis_index("ctx")
     dp = lax.axis_index("dp")
@@ -406,6 +406,8 @@
         return carry
 
     lax.fori_loop(0, tiles, gate_tile, 0)
+    gate_store = pltpu.make_async_copy(gate_ref, gate_hbm, store_sem.at[0])
+    gate_store.start()
 
     def own_sum(hop):
         total = term(chip((z + hop) % NZ, y, x))
@@ -455,6 +457,11 @@
         ig_copy(hop).wait_recv()
         ig_ref[:, columns] += ig_recv[:, columns]
 
+    def ig_store(at, hop):
+        columns = ig_columns(hop)
+        src, dst = ig_ref.at[:, columns], ig_hbm.at[:, columns]
+        return pltpu.make_async_copy(src, dst, store_sem.at[2 + at])
+
     ig_part(0)
     ig_part(near)
     ig_part(second)
@@ -470,9 +477,16 @@
     ig_part(last)
     wg_copy.wait_recv()
     wg_ref[:, other_half] = wg_recv[...]
-    for hop in (0, near, second, last):
+    wg_store = pltpu.make_async_copy(wg_ref, wg_hbm, store_sem.at[1])
+    wg_store.start()
+    for at, hop in enumerate((0, near, second, last)):
         ig_finish(hop)
-
+        ig_store(at, hop).start()
+
+    gate_store.wait()
+    wg_store.wait()
+    for at, hop in enumerate((0, near, second, last)):
+        ig_store(at, hop).wait()
     for single in (in_copy, back_copy, fwd_copy, val_copy, wg_copy):
         single.wait_send()
 
@@ -490,19 +504,24 @@
         ag_pf().wait_send()
 
 
-def write_kernel(ig_ref, gate_ref, wg_ref, ig_out, gate_out, wg_out, sems):
-    pairs = ((ig_ref, ig_out.at[0]), (gate_ref, gate_out.at[0]), (wg_ref, wg_out))
-    moves = []
+def write_kernel(ig_ref, gate_ref, wg_ref, ig_out, gate_out, wg_out, held, sems):
+    pairs = ((gate_ref, gate_out.at[0]), (wg_ref, wg_out), (ig_ref, ig_out.at[0]))
+    reads, writes = [], []
     for which, (src, dst) in enumerate(pairs):
         part = src.shape[0] // WRITES
         for at in range(WRITES):
             rows = pl.ds(at * part, part)
-            sem = sems.at[which * WRITES + at]
-            moves.append(pltpu.make_async_copy(src.at[rows, :], dst.at[rows, :], sem))
-    for move in moves:
-        move.start()
-    for move in moves:
-        move.wait()
+            stage = held.at[which, rows, :]
+            index = which * WRITES + at
+            reads.append(pltpu.make_async_copy(src.at[rows, :], stage, sems.at[0, index]))
+            writes.append(pltpu.make_async_copy(stage, dst.at[rows, :], sems.at[1, index]))
+    for read in reads:
+        read.start()
+    for read, write in zip(reads, writes):
+        read.wait()
+        write.start()
+    for write in writes:
+        write.wait()
 
 
 def written(in_grad, gate_grad, weight_grad):
@@ -516,7 +535,10 @@
         ),
         in_specs=[anywhere] * 3,
         out_specs=(anywhere,) * 3,
-        scratch_shapes=[pltpu.SemaphoreType.DMA((3 * WRITES,))],
+        scratch_shapes=[
+            pltpu.VMEM((3,) + in_grad.shape, F32),
+            pltpu.SemaphoreType.DMA((2, 3 * WRITES)),
+        ],
     )(in_grad, gate_grad, weight_grad)
 
 
@@ -541,8 +563,11 @@
             jax.ShapeDtypeStruct((block, channels), F32),
         ),
         in_specs=[pl.BlockSpec(memory_space=pl.ANY)] * 5 + [vmem] * 2,
-        out_specs=(vmem,) * 3,
+        out_specs=(pl.BlockSpec(memory_space=pl.ANY),) * 3,
         scratch_shapes=[
+            pltpu.VMEM((rows, width), F32),
+            pltpu.VMEM((rows, channels), F32),
+            pltpu.VMEM((block, channels), F32),
             pltpu.VMEM((rows, channels), BF16),
             pltpu.VMEM((rows, channels), BF16),
             pltpu.VMEM((rows, channels), BF16),
@@ -560,9 +585,10 @@
             pltpu.SemaphoreType.DMA((COPIES,)),
             pltpu.SemaphoreType.DMA((COPIES,)),
             pltpu.SemaphoreType.DMA((5,)),
+            pltpu.SemaphoreType.DMA((2 + NZ,)),
         ],
         compiler_params=pltpu.CompilerParams(
-            collective_id=0, has_side_effects=True, vmem_limit_bytes=40 * 1024 * 1024
+            collective_id=0, has_side_effects=True, vmem_limit_bytes=56 * 1024 * 1024
         ),
     )(inputs[0], values[0], gating[0], out_grad[0], weight, decay_rate, mode_gain)
     return written(in_grad, gate_grad, weight_grad)

time: 178 us -> 76 us (0.43)
  Pallas kernels: 167 us -> 75.2 us
  local copies, waits for them, and re-layouts: 9.98 us -> 0 us
    pallas_call x1, Pallas kernels: 96.5 us -> 2.81 us  [written(): pl.pallas_call(write_kernel, out_shape=(jax.ShapeDtypeStruct((1,) + in_gr...]
    unnamed x20 -> x0, local copies, waits for them, and re-layouts: 9.98 us -> none
    pallas_call x1, Pallas kernels: 70.6 us -> 72.4 us  [on_chip_grid(): pl.pallas_call(functools.partial(chip_kernel, scale), out_shape=(jax.Shap...]
where the time goes in v7:
time: 76 us; the launch traced here: 75.9 us
  Pallas kernels  75.2 us (99%)
    pallas_call x1, Pallas kernels, on_chip_grid(): pl.pallas_call(functools.partial(chip_kernel, scale), out_shape=(jax.Shap...  72.4 us
    pallas_call x1, Pallas kernels, written(): pl.pallas_call(write_kernel, out_shape=(jax.ShapeDtypeStruct((1,) + in_gr...  2.81 us

profile of v7, /device:TPU:1, one launch (start us, length us, event | category | flops | bytes accessed | tf_op | source)
XLA Modules:
  0.0 75.9 jit_solution(14237481086422128577)
XLA Ops:
  0.6 72.4 %shard_map.94 = (f32[128,2048]{1,0:T(8,128)}, f32[128,2048]{1,0:T(8,128)}, f32[128,2048]{1,0:T(8,128)}) custom-call(bf16[128,2048]{1,0:T(8,128)(2,1)} %bitcast.4, bf16[128,2048]{1,0:T(8,128)(2,1)} %bitcast.5, bf16[128,2048]{1,0:T(8,128)(2,1)} %bitcast.6, bf16[128,2048]{1,0:T(8,128)(2,1)} %bitcast.7, bf16[128,2048]{1,0:T(8,128)(2,1)} %weight_hbm.1, ...), custom_call_target="tpu_custom_call" | custom-call | tf_op jit(solution)/shard_map/pallas_call | solution.py:558
  73.1 2.8 %shard_map.95 = (f32[1,128,2048]{2,1,0:T(8,128)}, f32[1,128,2048]{2,1,0:T(8,128)}, f32[128,2048]{1,0:T(8,128)}) custom-call(f32[128,2048]{1,0:T(8,128)} %get-tuple-element.6.ig_ref, f32[128,2048]{1,0:T(8,128)} %get-tuple-element.7.gate_ref, f32[128,2048]{1,0:T(8,128)} %get-tuple-element.8.wg_ref), custom_call_target="tpu_custom_call" | custom-call | tf_op jit(solution)/shard_map/pallas_call | solution.py:529

commit v8 on v7

--- a/solution.py
+++ b/solution.py
@@ -424,8 +424,8 @@
     rs_third(2)
     ag_third(second)
     rs_third(3)
+    ag_third(last)
     wg_send[...] = own_sum(0)
-    ag_third(last)
 
     def ig_columns(hop):
         first = ((z - hop + NZ) % NZ) * 4 * block

time: 76 us -> 76 us (level)
  no operation moved by 1% of the time
where the time goes in v8:
time: 76 us; the launch traced here: 75.9 us
  Pallas kernels  75.2 us (99%)
    pallas_call x1, Pallas kernels, on_chip_grid(): pl.pallas_call(functools.partial(chip_kernel, scale), out_shape=(jax.Shap...  72.4 us
    pallas_call x1, Pallas kernels, written(): pl.pallas_call(write_kernel, out_shape=(jax.ShapeDtypeStruct((1,) + in_gr...  2.81 us

profile of v8, /device:TPU:1, one launch (start us, length us, event | category | flops | bytes accessed | tf_op | source)
XLA Modules:
  0.0 75.9 jit_solution(1798453033281578907)
XLA Ops:
  0.6 72.4 %shard_map.94 = (f32[128,2048]{1,0:T(8,128)}, f32[128,2048]{1,0:T(8,128)}, f32[128,2048]{1,0:T(8,128)}) custom-call(bf16[128,2048]{1,0:T(8,128)(2,1)} %bitcast.4, bf16[128,2048]{1,0:T(8,128)(2,1)} %bitcast.5, bf16[128,2048]{1,0:T(8,128)(2,1)} %bitcast.6, bf16[128,2048]{1,0:T(8,128)(2,1)} %bitcast.7, bf16[128,2048]{1,0:T(8,128)(2,1)} %weight_hbm.1, ...), custom_call_target="tpu_custom_call" | custom-call | tf_op jit(solution)/shard_map/pallas_call | solution.py:558
  73.1 2.8 %shard_map.95 = (f32[1,128,2048]{2,1,0:T(8,128)}, f32[1,128,2048]{2,1,0:T(8,128)}, f32[128,2048]{1,0:T(8,128)}) custom-call(f32[128,2048]{1,0:T(8,128)} %get-tuple-element.6.ig_ref, f32[128,2048]{1,0:T(8,128)} %get-tuple-element.7.gate_ref, f32[128,2048]{1,0:T(8,128)} %get-tuple-element.8.wg_ref), custom_call_target="tpu_custom_call" | custom-call | tf_op jit(solution)/shard_map/pallas_call | solution.py:529
